TPU v7x, 512 devices: a whole 4x4x16 slice. The times are simulated.
512 devices in a mesh: section: 16 (over z), expert: 32 (over y, x, core).
Axes of the slice: x: 4, y: 4, z: 16, core: 2. Of those that a mesh axis runs over, the one named last changes fastest.
Arguments:
- fwd_in: bfloat16 [16, 256, 3584], P('section', 'expert'), may hold values from -6 to 6
- fwd_enter: bfloat16 [1, 256, 3584], P(None, 'expert'), may hold values from -6 to 6
- bwd_in: bfloat16 [16, 256, 3584], P('section', 'expert'), may hold values from -6 to 6
- bwd_enter: bfloat16 [1, 256, 3584], P(None, 'expert'), may hold values from -6 to 6
- saved: bfloat16 [16, 2, 256, 3584], P('section', None, 'expert'), may hold values from -6 to 6
- fwd_routes: int32 [16, 2, 256, 2], P('section'), may hold values from 0 to 3, all different within a row; in each aligned block of 8 rows (0 to 7, 8 to 15, ..., all dimensions but the last counted through in order) at most 6 rows name the same one
- fwd_gates: float32 [16, 2, 256, 2], P('section'), may hold values from 0.2 to 1
- bwd_routes: int32 [16, 2, 256, 2], P('section'), may hold values from 0 to 3, all different within a row; in each aligned block of 8 rows (0 to 7, 8 to 15, ..., all dimensions but the last counted through in order) at most 6 rows name the same one
- bwd_gates: float32 [16, 2, 256, 2], P('section'), may hold values from 0.2 to 1
- gain: float32 [16, 3584], P('section'), may hold values from 0.5 to 1.5
- w_gate: bfloat16 [16, 3584, 4096], P('section', None, 'expert'), may hold values from -0.09375 to 0.09375
- w_up: bfloat16 [16, 3584, 4096], P('section', None, 'expert'), may hold values from -0.09375 to 0.09375
- w_down: bfloat16 [16, 4096, 3584], P('section', 'expert'), may hold values from -0.1875 to 0.1875
Outputs:
- fwd_out: bfloat16 [16, 2, 256, 3584], P('section', None, 'expert')
- bwd_out: bfloat16 [16, 2, 256, 3584], P('section', None, 'expert')
Inputs may be any that keep to these rules, and one draw needn't show every extreme that they name: `fwd_routes`: in each aligned block of 8 rows (the tokens of one device) a row names 2 different experts and no expert is named by more than 6 rows; some expert is named by exactly 6 rows in some block. `bwd_routes`: in each aligned block of 8 rows (the tokens of one device) a row names 2 different experts and no expert is named by more than 6 rows; some expert is named by exactly 6 rows in some block.
All inputs are finite; a program needn't handle non-finite values.
Results may differ from a plain program's by a relative error of at most 0.0095.
Values may be sent and summed in bfloat16 or wider, within the bound.
A program may use at most 64 MiB of HBM per device.

v0:
```python
import jax
import jax.numpy as jnp
from jax import lax
from jax.sharding import PartitionSpec as P

EXPERTS = 4
STEPS = 2
CAP = 6


EPSILON = 1e-06
PRECISE = lax.Precision.HIGHEST


def passed_along(value, axis, steps):
    count = lax.axis_size(axis)
    first, last = (max(0, -steps), min(count, count - steps))
    return lax.ppermute(value, axis, [(source, source + steps) for source in range(first, last)])


def normalize(inputs, scale_gain):
    scale = lax.rsqrt(jnp.mean(inputs * inputs, axis=-1, keepdims=True) + EPSILON)
    return (scale, (inputs * scale * scale_gain).astype(jnp.bfloat16))


def slot_table(routes, experts, capacity):
    labels = jnp.arange(experts, dtype=jnp.int32)
    hits = (routes[:, :, None] == labels[None, None, :]).astype(jnp.int32)
    flat = hits.reshape(-1, experts)
    before = jnp.cumsum(flat, axis=0) - flat
    slots = jnp.sum(before * flat, axis=1).reshape(routes.shape)
    places = (slots[None, :, :] == jnp.arange(capacity, dtype=jnp.int32)[:, None, None]).astype(
        jnp.float32
    )
    return jnp.transpose(hits, (2, 0, 1)).astype(jnp.float32)[:, None] * places[None]


def spread(block, groups):
    experts, capacity, width = block.shape
    return jnp.broadcast_to(block[:, None], (experts, groups, capacity, width)).reshape(
        experts * groups, capacity, width
    )


def expert_forward(rows, w_gate, w_up, w_down):
    flat = rows.reshape(-1, rows.shape[-1])
    gate_pre = jnp.dot(flat, w_gate, preferred_element_type=jnp.float32)
    up_pre = jnp.dot(flat, w_up, preferred_element_type=jnp.float32)
    hidden = (jax.nn.silu(gate_pre) * up_pre).astype(jnp.bfloat16)
    result = jnp.dot(hidden, w_down, preferred_element_type=jnp.float32).astype(jnp.bfloat16)
    return result.reshape(rows.shape)


def expert_backward(rows, grads, w_gate, w_up, w_down):
    width = rows.shape[-1]
    flat = rows.reshape(-1, width)
    upstream = grads.reshape(-1, width)
    contract = (((1,), (1,)), ((), ()))
    gate_pre = jnp.dot(flat, w_gate, preferred_element_type=jnp.float32)
    up_pre = jnp.dot(flat, w_up, preferred_element_type=jnp.float32)
    sigma = jax.nn.sigmoid(gate_pre)
    d_hidden = lax.dot_general(upstream, w_down, contract, preferred_element_type=jnp.float32)
    d_gate = (d_hidden * up_pre * sigma * (1.0 + gate_pre * (1.0 - sigma))).astype(jnp.bfloat16)
    d_up = (d_hidden * gate_pre * sigma).astype(jnp.bfloat16)
    result = lax.dot_general(d_gate, w_gate, contract, preferred_element_type=jnp.float32)
    result = result + lax.dot_general(d_up, w_up, contract, preferred_element_type=jnp.float32)
    return result.astype(jnp.bfloat16).reshape(rows.shape)


def per_device(
    fwd_in,
    fwd_enter,
    bwd_in,
    bwd_enter,
    saved,
    fwd_routes,
    fwd_gates,
    bwd_routes,
    bwd_gates,
    gain,
    w_gate,
    w_up,
    w_down,
):
    rows_dev = fwd_in.shape[1]
    devices = lax.axis_size("expert")
    groups = devices // EXPERTS
    place = lax.axis_index("expert")
    section_at = lax.axis_index("section")
    last_section = lax.axis_size("section") - 1
    scale_gain = gain[0]
    gate_shard = w_gate[0]
    up_shard = w_up[0]
    down_shard = w_down[0]
    width = gate_shard.shape[0]
    carry_forward = fwd_in[0]
    carry_backward = bwd_in[0]
    forward_list = []
    backward_list = []
    for step in range(STEPS):
        routes_forward = fwd_routes[0, step]
        routes_backward = bwd_routes[0, step]
        gates_forward = fwd_gates[0, step]
        gates_backward = bwd_gates[0, step]
        own_routes_f = lax.dynamic_slice_in_dim(routes_forward, place * rows_dev, rows_dev, 0)
        own_gates_f = lax.dynamic_slice_in_dim(gates_forward, place * rows_dev, rows_dev, 0)
        own_routes_b = lax.dynamic_slice_in_dim(routes_backward, place * rows_dev, rows_dev, 0)
        own_gates_b = lax.dynamic_slice_in_dim(gates_backward, place * rows_dev, rows_dev, 0)
        forward_x = carry_forward.astype(jnp.float32)
        forward_scale, normed_f = normalize(forward_x, scale_gain)
        table_f = slot_table(own_routes_f, EXPERTS, CAP)
        weighted_f = jnp.sum(table_f * own_gates_f[None, None], axis=-1)
        backward_x = saved[0, step].astype(jnp.float32)
        backward_scale, normed_b = normalize(backward_x, scale_gain)
        upstream = carry_backward.astype(jnp.float32)
        table_b = slot_table(own_routes_b, EXPERTS, CAP)
        picked_b = jnp.sum(table_b, axis=-1)
        weighted_b = jnp.sum(table_b * own_gates_b[None, None], axis=-1)
        picked_f = jnp.sum(table_f, axis=-1).astype(jnp.bfloat16)
        send_f = jnp.einsum(
            "eci,id->ecd", picked_f, normed_f, preferred_element_type=jnp.float32
        ).astype(jnp.bfloat16)
        answer_f = expert_forward(
            lax.all_to_all(
                spread(send_f, groups), "expert", split_axis=0, concat_axis=0, tiled=True
            ),
            gate_shard,
            up_shard,
            down_shard,
        )
        send_rows = jnp.einsum(
            "eci,id->ecd",
            picked_b.astype(jnp.bfloat16),
            normed_b,
            preferred_element_type=jnp.float32,
        ).astype(jnp.bfloat16)
        send_grads = jnp.einsum("eci,id->ecd", weighted_b, upstream, precision=PRECISE).astype(
            jnp.bfloat16
        )
        answer_b = expert_backward(
            lax.all_to_all(
                spread(send_rows, groups), "expert", split_axis=0, concat_axis=0, tiled=True
            ),
            lax.all_to_all(
                spread(send_grads, groups), "expert", split_axis=0, concat_axis=0, tiled=True
            ),
            gate_shard,
            up_shard,
            down_shard,
        )
        back_f = lax.all_to_all(answer_f, "expert", split_axis=0, concat_axis=0, tiled=True)
        back_b = lax.all_to_all(answer_b, "expert", split_axis=0, concat_axis=0, tiled=True)
        total_f = jnp.sum(back_f.reshape(EXPERTS, groups, CAP, width).astype(jnp.float32), axis=1)
        mixed = jnp.einsum("eci,ecd->id", weighted_f, total_f, precision=PRECISE)
        layer_out = (forward_x + mixed).astype(jnp.bfloat16)
        total_b = jnp.sum(back_b.reshape(EXPERTS, groups, CAP, width).astype(jnp.float32), axis=1)
        d_normed = jnp.einsum("eci,ecd->id", picked_b, total_b, precision=PRECISE)
        product = d_normed * scale_gain
        change = backward_scale * product - backward_x * backward_scale**3 * jnp.mean(
            product * backward_x, axis=-1, keepdims=True
        )
        input_grad = (upstream + change).astype(jnp.bfloat16)
        forward_list.append(layer_out)
        backward_list.append(input_grad)
        if step + 1 < STEPS:
            moved_forward = passed_along(layer_out, "section", 1)
            carry_forward = jnp.where(section_at == 0, fwd_enter[step], moved_forward)
            moved_backward = passed_along(input_grad, "section", -1)
            carry_backward = jnp.where(section_at == last_section, bwd_enter[step], moved_backward)
    return (jnp.stack(forward_list)[None], jnp.stack(backward_list)[None])


def solution(mesh):
    in_specs = (
        P("section", "expert", None),
        P(None, "expert", None),
        P("section", "expert", None),
        P(None, "expert", None),
        P("section", None, "expert", None),
        P("section", None, None, None),
        P("section", None, None, None),
        P("section", None, None, None),
        P("section", None, None, None),
        P("section", None),
        P("section", None, "expert"),
        P("section", None, "expert"),
        P("section", "expert", None),
    )
    out_specs = (P("section", None, "expert", None), P("section", None, "expert", None))
    return jax.shard_map(
        per_device, mesh=mesh, in_specs=in_specs, out_specs=out_specs, check_vma=False
    )
```

profile of v0, /device:TPU:1, one launch (start us, length us, event | category | flops | bytes accessed | tf_op | source)
XLA Modules:
  0.0 336.4 jit_solution(6462211872096117113)
XLA Ops:
  6.7 10.7 %all-to-all-start.4 = ((bf16[32,6,3584]{2,1,0:T(8,128)(2,1)}), bf16[32,6,3584]{2,1,0:T(8,128)(2,1)S(1)}, u32[]{:S(2)}, u32[]{:S(2)}) async-start(bf16[32,6,3584]{2,1,0:T(8,128)(2,1)} %bitcast.181), calls=%async_computation.4 | async-start | bytes 3670016 | tf_op jit(solution)/shard_map/all_to_all | solution.py:144
  18.9 23.4 %all-to-all-done.4 = bf16[32,6,3584]{2,1,0:T(8,128)(2,1)S(1)} async-done(((bf16[32,6,3584]{2,1,0:T(8,128)(2,1)}), bf16[32,6,3584]{2,1,0:T(8,128)(2,1)S(1)}, u32[]{:S(2)}, u32[]{:S(2)}) %all-to-all-start.4) | async-done | bytes 1376288 | tf_op jit(solution)/shard_map/all_to_all | solution.py:144
  43.7 6.7 %all-to-all-start.5 = ((bf16[32,6,3584]{2,1,0:T(8,128)(2,1)}), bf16[32,6,3584]{2,1,0:T(8,128)(2,1)}, u32[]{:S(2)}, u32[]{:S(2)}) async-start(bf16[32,6,3584]{2,1,0:T(8,128)(2,1)} %bitcast.180), calls=%async_computation.5 | async-start | bytes 3670016 | tf_op jit(solution)/shard_map/all_to_all | solution.py:141
  51.9 23.6 %all-to-all-done.5 = bf16[32,6,3584]{2,1,0:T(8,128)(2,1)} async-done(((bf16[32,6,3584]{2,1,0:T(8,128)(2,1)}), bf16[32,6,3584]{2,1,0:T(8,128)(2,1)}, u32[]{:S(2)}, u32[]{:S(2)}) %all-to-all-start.5) | async-done | bytes 1376288 | tf_op jit(solution)/shard_map/all_to_all | solution.py:141
  76.9 6.6 %all-to-all-start = ((bf16[32,6,3584]{2,1,0:T(8,128)(2,1)}), bf16[32,6,3584]{2,1,0:T(8,128)(2,1)}, u32[]{:S(2)}, u32[]{:S(2)}) async-start(bf16[32,6,3584]{2,1,0:T(8,128)(2,1)} %bitcast.183), calls=%async_computation | async-start | bytes 3670016 | tf_op jit(solution)/shard_map/all_to_all | solution.py:124
  85.2 3.6 %reshape.209 = bf16[192,3584]{1,0:T(8,128)(2,1)} reshape(bf16[32,6,3584]{2,1,0:T(8,128)(2,1)} %all-to-all-done.5) | data formatting | bytes 2752512 | tf_op jit(solution)/shard_map/reshape | solution.py:56
  91.3 3.9 %fusion.18 = f32[192,3584]{1,0:T(8,128)} fusion(f32[192,128]{1,0:T(8,128)S(1)} %fusion.21, bf16[192,3584]{1,0:T(8,128)(2,1)} %reshape.209, bf16[1,3584,128]{2,1,0:T(8,128)(2,1)S(1)} %copy-done, bf16[1,3584,128]{2,1,0:T(8,128)(2,1)S(1)} %copy-done.1, f32[192,128]{1,0:T(8,128)S(1)} %fusion.39), kind=kOutput, calls=%fused_computation.40 | convolution fusion | flops 352567296 | bytes 6160384 | tf_op jit(solution)/shard_map/dot_general | solution.py:65
  95.2 3.4 %fusion = bf16[192,3584]{1,0:T(8,128)(2,1)} fusion(f32[192,3584]{1,0:T(8,128)} %fusion.18, bf16[1,3584,128]{2,1,0:T(8,128)(2,1)S(1)} %copy-done, f32[192,128]{1,0:T(8,128)S(1)} %fusion.21, f32[192,128]{1,0:T(8,128)S(1)} %fusion.39), kind=kOutput, calls=%fused_computation.2 | convolution fusion | flops 177684480 | bytes 5242880 | tf_op jit(solution)/shard_map/dot_general | solution.py:66
  98.5 3.4 %reshape.210 = bf16[32,6,3584]{2,1,0:T(8,128)(2,1)} reshape(bf16[192,3584]{1,0:T(8,128)(2,1)} %fusion) | data formatting | bytes 2752512 | tf_op jit(solution)/shard_map/reshape | solution.py:67
  101.9 6.6 %all-to-all-done = bf16[32,6,3584]{2,1,0:T(8,128)(2,1)} async-done(((bf16[32,6,3584]{2,1,0:T(8,128)(2,1)}), bf16[32,6,3584]{2,1,0:T(8,128)(2,1)}, u32[]{:S(2)}, u32[]{:S(2)}) %all-to-all-start) | async-done | bytes 1376288 | tf_op jit(solution)/shard_map/all_to_all | solution.py:124
  108.5 6.6 %all-to-all-start.6 = ((bf16[32,6,3584]{2,1,0:T(8,128)(2,1)}), bf16[32,6,3584]{2,1,0:T(8,128)(2,1)}, u32[]{:S(2)}, u32[]{:S(2)}) async-start(bf16[32,6,3584]{2,1,0:T(8,128)(2,1)} %reshape.210), calls=%async_computation.6 | async-start | bytes 3670016 | tf_op jit(solution)/shard_map/all_to_all | solution.py:152
  115.6 3.5 %reshape.201 = bf16[192,3584]{1,0:T(8,128)(2,1)} reshape(bf16[32,6,3584]{2,1,0:T(8,128)(2,1)} %all-to-all-done) | data formatting | bytes 2752512 | tf_op jit(solution)/shard_map/reshape | solution.py:46
  121.0 3.5 %convolution_convert_fusion.1 = bf16[192,3584]{1,0:T(8,128)(2,1)} fusion(bf16[192,3584]{1,0:T(8,128)(2,1)} %reshape.201, bf16[1,128,3584]{2,1,0:T(8,128)(2,1)S(1)} %copy-done.2, bf16[1,3584,128]{2,1,0:T(8,128)(2,1)S(1)} %copy-done, f32[192,128]{1,0:T(8,128)S(1)} %fusion.43), kind=kOutput, calls=%fused_computation.5 | convolution fusion | flops 353157120 | bytes 4685824 | tf_op jit(solution)/shard_map/dot_general | solution.py:50
  127.8 12.4 %all-to-all-done.6 = bf16[32,6,3584]{2,1,0:T(8,128)(2,1)} async-done(((bf16[32,6,3584]{2,1,0:T(8,128)(2,1)}), bf16[32,6,3584]{2,1,0:T(8,128)(2,1)}, u32[]{:S(2)}, u32[]{:S(2)}) %all-to-all-start.6) | async-done | bytes 1376288 | tf_op jit(solution)/shard_map/all_to_all | solution.py:152
  140.2 6.6 %all-to-all-start.1 = ((bf16[32,6,3584]{2,1,0:T(8,128)(2,1)}), bf16[32,6,3584]{2,1,0:T(8,128)(2,1)}, u32[]{:S(2)}, u32[]{:S(2)}) async-start(bf16[32,6,3584]{2,1,0:T(8,128)(2,1)} %reshape.202), calls=%async_computation.1 | async-start | bytes 3670016 | tf_op jit(solution)/shard_map/all_to_all | solution.py:151
  151.3 20.5 %all-to-all-done.1 = bf16[32,6,3584]{2,1,0:T(8,128)(2,1)} async-done(((bf16[32,6,3584]{2,1,0:T(8,128)(2,1)}), bf16[32,6,3584]{2,1,0:T(8,128)(2,1)}, u32[]{:S(2)}, u32[]{:S(2)}) %all-to-all-start.1) | async-done | bytes 1376288 | tf_op jit(solution)/shard_map/all_to_all | solution.py:151
  173.2 6.7 %all-to-all-start.8 = ((bf16[32,6,3584]{2,1,0:T(8,128)(2,1)}), bf16[32,6,3584]{2,1,0:T(8,128)(2,1)}, u32[]{:S(2)}, u32[]{:S(2)}) async-start(bf16[32,6,3584]{2,1,0:T(8,128)(2,1)} %bitcast.182), calls=%async_computation.8 | async-start | bytes 3670016 | tf_op jit(solution)/shard_map/all_to_all | solution.py:141
  182.0 3.4 %collective-permute-done.1 = bf16[8,3584]{1,0:T(8,128)(2,1)S(1)} collective-permute-done((bf16[8,3584]{1,0:T(8,128)(2,1)S(1)}, bf16[8,3584]{1,0:T(8,128)(2,1)S(1)}, u32[]{:S(2)}, u32[]{:S(2)}) %collective-permute-start.1) | collective-permute-done | bytes 57376 | tf_op jit(solution)/shard_map/ppermute | solution.py:18
  185.8 19.2 %all-to-all-done.8 = bf16[32,6,3584]{2,1,0:T(8,128)(2,1)} async-done(((bf16[32,6,3584]{2,1,0:T(8,128)(2,1)}), bf16[32,6,3584]{2,1,0:T(8,128)(2,1)}, u32[]{:S(2)}, u32[]{:S(2)}) %all-to-all-start.8) | async-done | bytes 1376288 | tf_op jit(solution)/shard_map/all_to_all | solution.py:141
  206.4 6.8 %all-to-all-start.7 = ((bf16[32,6,3584]{2,1,0:T(8,128)(2,1)}), bf16[32,6,3584]{2,1,0:T(8,128)(2,1)}, u32[]{:S(2)}, u32[]{:S(2)}) async-start(bf16[32,6,3584]{2,1,0:T(8,128)(2,1)} %bitcast.179), calls=%async_computation.7 | async-start | bytes 3670016 | tf_op jit(solution)/shard_map/all_to_all | solution.py:144
  219.1 19.1 %all-to-all-done.7 = bf16[32,6,3584]{2,1,0:T(8,128)(2,1)} async-done(((bf16[32,6,3584]{2,1,0:T(8,128)(2,1)}), bf16[32,6,3584]{2,1,0:T(8,128)(2,1)}, u32[]{:S(2)}, u32[]{:S(2)}) %all-to-all-start.7) | async-done | bytes 1376288 | tf_op jit(solution)/shard_map/all_to_all | solution.py:144
  239.6 6.6 %all-to-all-start.2 = ((bf16[32,6,3584]{2,1,0:T(8,128)(2,1)}), bf16[32,6,3584]{2,1,0:T(8,128)(2,1)}, u32[]{:S(2)}, u32[]{:S(2)}) async-start(bf16[32,6,3584]{2,1,0:T(8,128)(2,1)} %bitcast.184), calls=%async_computation.2 | async-start | bytes 3670016 | tf_op jit(solution)/shard_map/all_to_all | solution.py:124
  246.2 3.5 %reshape.214 = bf16[192,3584]{1,0:T(8,128)(2,1)} reshape(bf16[32,6,3584]{2,1,0:T(8,128)(2,1)} %all-to-all-done.8) | data formatting | bytes 2752512 | tf_op jit(solution)/shard_map/reshape | solution.py:56
  251.6 3.5 %reshape.212 = bf16[192,3584]{1,0:T(8,128)(2,1)} reshape(bf16[32,6,3584]{2,1,0:T(8,128)(2,1)} %all-to-all-done.7) | data formatting | bytes 2752512 | tf_op jit(solution)/shard_map/reshape | solution.py:57
  257.0 3.9 %fusion.17 = f32[192,3584]{1,0:T(8,128)} fusion(f32[192,128]{1,0:T(8,128)S(1)} %fusion.19, bf16[192,3584]{1,0:T(8,128)(2,1)} %reshape.214, bf16[1,3584,128]{2,1,0:T(8,128)(2,1)S(1)} %copy-done, bf16[1,3584,128]{2,1,0:T(8,128)(2,1)S(1)} %copy-done.1, f32[192,128]{1,0:T(8,128)S(1)} %fusion.36), kind=kOutput, calls=%fused_computation.39 | convolution fusion | flops 352567296 | bytes 6160384 | tf_op jit(solution)/shard_map/dot_general | solution.py:65
  260.8 3.5 %fusion.1 = bf16[192,3584]{1,0:T(8,128)(2,1)} fusion(f32[192,3584]{1,0:T(8,128)} %fusion.17, bf16[1,3584,128]{2,1,0:T(8,128)(2,1)S(1)} %copy-done, f32[192,128]{1,0:T(8,128)S(1)} %fusion.19, f32[192,128]{1,0:T(8,128)S(1)} %fusion.36), kind=kOutput, calls=%fused_computation.3 | convolution fusion | flops 177684480 | bytes 5242880 | tf_op jit(solution)/shard_map/dot_general | solution.py:66
  267.7 3.6 %all-to-all-done.2 = bf16[32,6,3584]{2,1,0:T(8,128)(2,1)} async-done(((bf16[32,6,3584]{2,1,0:T(8,128)(2,1)}), bf16[32,6,3584]{2,1,0:T(8,128)(2,1)}, u32[]{:S(2)}, u32[]{:S(2)}) %all-to-all-start.2) | async-done | bytes 1376288 | tf_op jit(solution)/shard_map/all_to_all | solution.py:124
  271.2 6.6 %all-to-all-start.9 = ((bf16[32,6,3584]{2,1,0:T(8,128)(2,1)}), bf16[32,6,3584]{2,1,0:T(8,128)(2,1)}, u32[]{:S(2)}, u32[]{:S(2)}) async-start(bf16[32,6,3584]{2,1,0:T(8,128)(2,1)} %reshape.215), calls=%async_computation.9 | async-start | bytes 3670016 | tf_op jit(solution)/shard_map/all_to_all | solution.py:152
  277.9 3.5 %reshape.204 = bf16[192,3584]{1,0:T(8,128)(2,1)} reshape(bf16[32,6,3584]{2,1,0:T(8,128)(2,1)} %all-to-all-done.2) | data formatting | bytes 2752512 | tf_op jit(solution)/shard_map/reshape | solution.py:46
  287.0 15.9 %all-to-all-done.9 = bf16[32,6,3584]{2,1,0:T(8,128)(2,1)} async-done(((bf16[32,6,3584]{2,1,0:T(8,128)(2,1)}), bf16[32,6,3584]{2,1,0:T(8,128)(2,1)}, u32[]{:S(2)}, u32[]{:S(2)}) %all-to-all-start.9) | async-done | bytes 1376288 | tf_op jit(solution)/shard_map/all_to_all | solution.py:152
  302.9 5.9 %all-to-all-start.3 = ((bf16[32,6,3584]{2,1,0:T(8,128)(2,1)}), bf16[32,6,3584]{2,1,0:T(8,128)(2,1)S(1)}, u32[]{:S(2)}, u32[]{:S(2)}) async-start(bf16[32,6,3584]{2,1,0:T(8,128)(2,1)} %reshape.205), calls=%async_computation.3 | async-start | bytes 3670016 | tf_op jit(solution)/shard_map/all_to_all | solution.py:151
  311.7 22.2 %all-to-all-done.3 = bf16[32,6,3584]{2,1,0:T(8,128)(2,1)S(1)} async-done(((bf16[32,6,3584]{2,1,0:T(8,128)(2,1)}), bf16[32,6,3584]{2,1,0:T(8,128)(2,1)S(1)}, u32[]{:S(2)}, u32[]{:S(2)}) %all-to-all-start.3) | async-done | bytes 1376288 | tf_op jit(solution)/shard_map/all_to_all | solution.py:151
  (154 shorter events, 56.4 us)
Async XLA Ops:
  0.6 90.7 %copy-start = (bf16[1,3584,128]{2,1,0:T(8,128)(2,1)S(1)}, bf16[1,3584,128]{2,1,0:T(8,128)(2,1)}, u32[]{:S(2)}) copy-start(bf16[1,3584,128]{2,1,0:T(8,128)(2,1)} %param.24) | copy-start | bytes 2752516
  6.7 10.7 %copy-start.20 = (s32[1,2,256,2]{2,3,1,0:T(2,128)S(1)}, s32[1,2,256,2]{2,3,1,0:T(2,128)}, u32[]{:S(2)}) copy-start(s32[1,2,256,2]{2,3,1,0:T(2,128)} %param.18) | copy-start | bytes 12292
  6.7 11.2 %copy-start.18 = (f32[1,3584]{1,0:T(1,128)S(1)}, f32[1,3584]{1,0:T(1,128)}, u32[]{:S(2)}) copy-start(f32[1,3584]{1,0:T(1,128)} %param.22) | copy-start | bytes 43012
  6.7 11.3 %copy-start.4 = (bf16[1,2,8,3584]{3,2,1,0:T(8,128)(2,1)S(1)}, bf16[1,2,8,3584]{3,2,1,0:T(8,128)(2,1)}, u32[]{:S(2)}) copy-start(bf16[1,2,8,3584]{3,2,1,0:T(8,128)(2,1)} %param.17) | copy-start | bytes 344068
  6.7 35.6 %all-to-all-start.4 = ((bf16[32,6,3584]{2,1,0:T(8,128)(2,1)}), bf16[32,6,3584]{2,1,0:T(8,128)(2,1)S(1)}, u32[]{:S(2)}, u32[]{:S(2)}) async-start(bf16[32,6,3584]{2,1,0:T(8,128)(2,1)} %bitcast.181), calls=%async_computation.4 | async-start | bytes 3670016 | tf_op jit(solution)/shard_map/all_to_all | solution.py:144
  18.7 25.1 %copy-start.24 = (f32[8]{0:T(128)}, f32[8]{0:T(128)S(1)}, u32[]{:S(2)}) copy-start(f32[8]{0:T(128)S(1)} %get-tuple-element.25) | copy-start | bytes 100
  43.7 7.8 %copy-start.5 = (bf16[1,8,3584]{2,1,0:T(8,128)(2,1)S(1)}, bf16[1,8,3584]{2,1,0:T(8,128)(2,1)}, u32[]{:S(2)}) copy-start(bf16[1,8,3584]{2,1,0:T(8,128)(2,1)} %param.13) | copy-start | bytes 172036
  43.7 31.8 %all-to-all-start.5 = ((bf16[32,6,3584]{2,1,0:T(8,128)(2,1)}), bf16[32,6,3584]{2,1,0:T(8,128)(2,1)}, u32[]{:S(2)}, u32[]{:S(2)}) async-start(bf16[32,6,3584]{2,1,0:T(8,128)(2,1)} %bitcast.180), calls=%async_computation.5 | async-start | bytes 3670016 | tf_op jit(solution)/shard_map/all_to_all | solution.py:141
  76.9 31.6 %all-to-all-start = ((bf16[32,6,3584]{2,1,0:T(8,128)(2,1)}), bf16[32,6,3584]{2,1,0:T(8,128)(2,1)}, u32[]{:S(2)}, u32[]{:S(2)}) async-start(bf16[32,6,3584]{2,1,0:T(8,128)(2,1)} %bitcast.183), calls=%async_computation | async-start | bytes 3670016 | tf_op jit(solution)/shard_map/all_to_all | solution.py:124
  85.2 3.6 %copy-start.2 = (bf16[1,128,3584]{2,1,0:T(8,128)(2,1)S(1)}, bf16[1,128,3584]{2,1,0:T(8,128)(2,1)}, u32[]{:S(2)}) copy-start(bf16[1,128,3584]{2,1,0:T(8,128)(2,1)} %param.25) | copy-start | bytes 2752516
  108.5 31.7 %all-to-all-start.6 = ((bf16[32,6,3584]{2,1,0:T(8,128)(2,1)}), bf16[32,6,3584]{2,1,0:T(8,128)(2,1)}, u32[]{:S(2)}, u32[]{:S(2)}) async-start(bf16[32,6,3584]{2,1,0:T(8,128)(2,1)} %reshape.210), calls=%async_computation.6 | async-start | bytes 3670016 | tf_op jit(solution)/shard_map/all_to_all | solution.py:152
  140.2 31.7 %all-to-all-start.1 = ((bf16[32,6,3584]{2,1,0:T(8,128)(2,1)}), bf16[32,6,3584]{2,1,0:T(8,128)(2,1)}, u32[]{:S(2)}, u32[]{:S(2)}) async-start(bf16[32,6,3584]{2,1,0:T(8,128)(2,1)} %reshape.202), calls=%async_computation.1 | async-start | bytes 3670016 | tf_op jit(solution)/shard_map/all_to_all | solution.py:151
  151.1 22.1 %copy-start.22 = (f32[8]{0:T(128)}, f32[8]{0:T(128)S(1)}, u32[]{:S(2)}) copy-start(f32[8]{0:T(128)S(1)} %get-tuple-element.23) | copy-start | bytes 100
  173.2 6.8 %copy-start.8 = (bf16[1,8,3584]{2,1,0:T(8,128)(2,1)S(1)}, bf16[1,8,3584]{2,1,0:T(8,128)(2,1)}, u32[]{:S(2)}) copy-start(bf16[1,8,3584]{2,1,0:T(8,128)(2,1)} %param.15) | copy-start | bytes 172036
  173.2 6.8 %copy-start.25 = (f32[8]{0:T(128)S(1)}, f32[8]{0:T(128)}, u32[]{:S(2)}) copy-start(f32[8]{0:T(128)} %copy-done.24) | copy-start | bytes 100
  173.2 6.8 %copy-start.27 = (f32[8]{0:T(128)S(1)}, f32[8]{0:T(128)}, u32[]{:S(2)}) copy-start(f32[8]{0:T(128)} %get-tuple-element.24) | copy-start | bytes 100
  173.2 8.2 %copy-start.19 = (s32[8,2]{0,1:T(2,128)S(1)}, s32[8,2]{0,1:T(2,128)}, u32[]{:S(2)}) copy-start(s32[8,2]{0,1:T(2,128)} %copy.48) | copy-start | bytes 196
  173.2 12.2 %copy-start.11 = (bf16[1,8,3584]{2,1,0:T(8,128)(2,1)S(1)}, bf16[1,8,3584]{2,1,0:T(8,128)(2,1)}, u32[]{:S(2)}) copy-start(bf16[1,8,3584]{2,1,0:T(8,128)(2,1)} %param.16) | copy-start | bytes 172036
  173.2 31.8 %all-to-all-start.8 = ((bf16[32,6,3584]{2,1,0:T(8,128)(2,1)}), bf16[32,6,3584]{2,1,0:T(8,128)(2,1)}, u32[]{:S(2)}, u32[]{:S(2)}) async-start(bf16[32,6,3584]{2,1,0:T(8,128)(2,1)} %bitcast.182), calls=%async_computation.8 | async-start | bytes 3670016 | tf_op jit(solution)/shard_map/all_to_all | solution.py:141
  180.1 5.3 %copy-start.9 = (bf16[8,3584]{1,0:T(8,128)(2,1)}, bf16[8,3584]{1,0:T(8,128)(2,1)S(1)}, u32[]{:S(2)}) copy-start(bf16[8,3584]{1,0:T(8,128)(2,1)S(1)} %fusion.61) | copy-start | bytes 172036
  180.1 5.3 %collective-permute-start.1 = (bf16[8,3584]{1,0:T(8,128)(2,1)S(1)}, bf16[8,3584]{1,0:T(8,128)(2,1)S(1)}, u32[]{:S(2)}, u32[]{:S(2)}) collective-permute-start(bf16[8,3584]{1,0:T(8,128)(2,1)S(1)} %fusion.61), channel_id=1, source_target_pairs={{32,0},{64,32},{96,64},{128,96},{160,128},{192,160},{224,192},{256... | collective-permute-start | bytes 172040 | tf_op jit(solution)/shard_map/ppermute | solution.py:18
  185.4 21.0 %copy-start.13 = (bf16[8,3584]{1,0:T(8,128)(2,1)}, bf16[8,3584]{1,0:T(8,128)(2,1)S(1)}, u32[]{:S(2)}) copy-start(bf16[8,3584]{1,0:T(8,128)(2,1)S(1)} %collective-permute-done.1) | copy-start | bytes 172036
  206.4 31.8 %all-to-all-start.7 = ((bf16[32,6,3584]{2,1,0:T(8,128)(2,1)}), bf16[32,6,3584]{2,1,0:T(8,128)(2,1)}, u32[]{:S(2)}, u32[]{:S(2)}) async-start(bf16[32,6,3584]{2,1,0:T(8,128)(2,1)} %bitcast.179), calls=%async_computation.7 | async-start | bytes 3670016 | tf_op jit(solution)/shard_map/all_to_all | solution.py:144
  213.2 4.2 %copy-start.17 = (f32[6,8,2]{1,2,0:T(2,128)S(1)}, f32[6,8,2]{1,2,0:T(2,128)}, u32[]{:S(2)}) copy-start(f32[6,8,2]{1,2,0:T(2,128)} %compare_convert_fusion.2) | copy-start | bytes 1156
  213.2 4.2 %copy-start.21 = (f32[8,2]{0,1:T(2,128)S(1)}, f32[8,2]{0,1:T(2,128)}, u32[]{:S(2)}) copy-start(f32[8,2]{0,1:T(2,128)} %get-tuple-element.35) | copy-start | bytes 196
  213.2 5.5 %copy-start.15 = (bf16[1,8,3584]{2,1,0:T(8,128)(2,1)S(1)}, bf16[1,8,3584]{2,1,0:T(8,128)(2,1)}, u32[]{:S(2)}) copy-start(bf16[1,8,3584]{2,1,0:T(8,128)(2,1)} %param.14) | copy-start | bytes 172036
  215.9 2.7 collective-permute-start
  239.6 31.6 %all-to-all-start.2 = ((bf16[32,6,3584]{2,1,0:T(8,128)(2,1)}), bf16[32,6,3584]{2,1,0:T(8,128)(2,1)}, u32[]{:S(2)}, u32[]{:S(2)}) async-start(bf16[32,6,3584]{2,1,0:T(8,128)(2,1)} %bitcast.184), calls=%async_computation.2 | async-start | bytes 3670016 | tf_op jit(solution)/shard_map/all_to_all | solution.py:124
  271.2 31.7 %all-to-all-start.9 = ((bf16[32,6,3584]{2,1,0:T(8,128)(2,1)}), bf16[32,6,3584]{2,1,0:T(8,128)(2,1)}, u32[]{:S(2)}, u32[]{:S(2)}) async-start(bf16[32,6,3584]{2,1,0:T(8,128)(2,1)} %reshape.215), calls=%async_computation.9 | async-start | bytes 3670016 | tf_op jit(solution)/shard_map/all_to_all | solution.py:152
  302.9 30.9 %all-to-all-start.3 = ((bf16[32,6,3584]{2,1,0:T(8,128)(2,1)}), bf16[32,6,3584]{2,1,0:T(8,128)(2,1)S(1)}, u32[]{:S(2)}, u32[]{:S(2)}) async-start(bf16[32,6,3584]{2,1,0:T(8,128)(2,1)} %reshape.205), calls=%async_computation.3 | async-start | bytes 3670016 | tf_op jit(solution)/shard_map/all_to_all | solution.py:151
  311.6 24.0 %copy-start.23 = (f32[8]{0:T(128)S(1)}, f32[8]{0:T(128)}, u32[]{:S(2)}) copy-start(f32[8]{0:T(128)} %copy-done.22) | copy-start | bytes 100
  311.6 24.0 %copy-start.26 = (f32[8]{0:T(128)S(1)}, f32[8]{0:T(128)}, u32[]{:S(2)}) copy-start(f32[8]{0:T(128)} %get-tuple-element.22) | copy-start | bytes 100
  (8 other events, 15.7 us)
where the time goes:
time: 339 us; the launch traced here: 336 us
  waiting for transfers between devices  171 us (50%)
  starting transfers between devices  72.6 us (21%)
  local copies, waits for them, and re-layouts  43.8 us (13%)
  matrix products  36 us (11%)
  other arithmetic  11.7 us (3%)
    all_to_all x2, waiting for transfers between devices, per_device(): lax.all_to_all(spread(send_rows, groups), 'expert', split_axis=0, concat_...  42.8 us
    all_to_all x2, waiting for transfers between devices, per_device(): lax.all_to_all(answer_f, 'expert', split_axis=0, concat_axis=0, tiled=True)  42.7 us
    all_to_all x2, waiting for transfers between devices, per_device(): lax.all_to_all(spread(send_grads, groups), 'expert', split_axis=0, concat...  42.6 us
    all_to_all x2, waiting for transfers between devices, per_device(): lax.all_to_all(answer_b, 'expert', split_axis=0, concat_axis=0, tiled=True)  28.3 us
    all_to_all x2, starting transfers between devices, per_device(): lax.all_to_all(spread(send_grads, groups), 'expert', split_axis=0, concat...  17.4 us
    all_to_all x2, starting transfers between devices, per_device(): lax.all_to_all(spread(send_rows, groups), 'expert', split_axis=0, concat_...  13.5 us
    all_to_all x2, starting transfers between devices, per_device(): lax.all_to_all(answer_b, 'expert', split_axis=0, concat_axis=0, tiled=True)  13.2 us
    all_to_all x2, starting transfers between devices, per_device(): lax.all_to_all(spread(send_f, groups), 'expert', split_axis=0, concat_axi...  13.2 us
  transfers between devices with their start and end apart: 12, of which 12 were waited for; matrix products, arithmetic and copies ran while one was open for 23% of the time, Pallas kernels for 0%

commit v1 on v0

v1 whole, which is shorter than its diff:
```python
import functools

import jax
import jax.numpy as jnp
from jax import lax
from jax.experimental import pallas as pl
from jax.experimental.pallas import tpu as pltpu
from jax.sharding import PartitionSpec as P

EPSILON = 1e-06
MESH = pl.DeviceIdType.MESH
SIDE = 4
CORES = 2
PEERS = (1, 2, 3)
TILE = 512
F32 = jnp.float32
BF16 = jnp.bfloat16


def normalize(inputs, gain):
    scale = lax.rsqrt(jnp.mean(inputs * inputs, axis=-1, keepdims=True) + EPSILON)
    return scale, (inputs * scale * gain).astype(BF16)


def relay_kernel(
    sections,
    fwd_in,
    fwd_enter,
    bwd_in,
    bwd_enter,
    saved,
    fwd_routes,
    fwd_gates,
    bwd_routes,
    bwd_gates,
    gain,
    w_gate,
    w_up,
    w_down,
    fwd_out,
    bwd_out,
    in_f,
    enter_f,
    in_b,
    enter_b,
    in_s,
    routes_f,
    gates_f,
    routes_b,
    gates_b,
    gain_v,
    w_in,
    w_back,
    gathered,
    partial,
    landed_one,
    middle,
    landed_two,
    hop_send,
    hop_land,
    pre_act,
    load_sem,
    weight_send,
    weight_recv,
    gather_send,
    gather_recv,
    reduce_send,
    reduce_recv,
    hop_send_sem,
    hop_recv_sem,
):
    width = gain.shape[-1]
    half = width // 2
    unit = w_down.shape[0]
    rows = in_f.shape[0]
    tokens = SIDE * SIDE * rows
    section = lax.axis_index("section")
    place = lax.axis_index("expert")
    core = lax.rem(place, CORES)
    x = lax.rem(place // CORES, SIDE)
    y = place // (CORES * SIDE)

    def device(dy=0, dx=0, dc=0, dz=0):
        at_y, at_x = lax.rem(y + dy, SIDE), lax.rem(x + dx, SIDE)
        at_c = lax.rem(core + dc, CORES)
        return (lax.rem(section + dz, sections), (at_y * SIDE + at_x) * CORES + at_c)

    sibling = device(dc=1)
    following, preceding = device(dz=1), device(dz=sections - 1)
    along_y = [device(dy=k) for k in PEERS]
    along_x = [device(dx=k) for k in PEERS]

    barrier = pltpu.get_barrier_semaphore()
    greeted = [sibling, following, preceding] + along_y + along_x
    for other in greeted:
        pl.semaphore_signal(barrier, inc=1, device_id=other, device_id_type=MESH)

    small = [
        (fwd_in.at[0], in_f),
        (gain, gain_v),
        (saved.at[0], in_s),
        (bwd_in.at[0], in_b),
        (fwd_routes, routes_f),
        (fwd_gates, gates_f),
        (bwd_routes, routes_b),
        (bwd_gates, gates_b),
        (fwd_enter.at[0], enter_f),
        (bwd_enter.at[0], enter_b),
    ]
    own_weights = [
        (w_gate, w_in.at[:, pl.ds(0, unit)]),
        (w_up, w_in.at[:, pl.ds(2 * unit, unit)]),
        (w_down, w_back.at[pl.ds(0, unit), :]),
    ]
    sibling_weights = [
        (w_gate, w_in.at[:, pl.ds(unit, unit)]),
        (w_up, w_in.at[:, pl.ds(3 * unit, unit)]),
        (w_down, w_back.at[pl.ds(unit, unit), :]),
    ]
    loads = [
        pltpu.make_async_copy(source, target, load_sem.at[i])
        for i, (source, target) in enumerate(small + own_weights)
    ]
    for load in loads:
        load.start()
    for load in loads[: len(small)]:
        load.wait()

    gain_row = gain_v[...]
    block = (x, y)
    _, normed = normalize(in_f[...].astype(F32), gain_row)
    gathered[0, x, y] = normed
    scales = []
    for step in range(2):
        scale, normed = normalize(in_s[step].astype(F32), gain_row)
        scales.append(scale)
        gathered[1 + 3 * step, x, y] = normed
    gathered[2, x, y] = in_b[...]

    pl.semaphore_wait(barrier, len(greeted))

    first, second = pl.ds(0, half), pl.ds(half, half)

    def gather_one(u):
        out = []
        for k in range(len(PEERS)):
            for part, (peers, columns) in enumerate(((along_y, first), (along_x, second))):
                spot = gathered.at[u, x, y, :, columns]
                out.append(remote(spot, spot, gather_send, gather_recv, (u, 0, part, k), peers[k]))
        return out

    def gather_two(u):
        out = []
        for k in range(len(PEERS)):
            spot = gathered.at[u, x, :, :, first]
            out.append(remote(spot, spot, gather_send, gather_recv, (u, 1, 0, k), along_x[k]))
            spot = gathered.at[u, :, y, :, second]
            out.append(remote(spot, spot, gather_send, gather_recv, (u, 1, 1, k), along_y[k]))
        return out

    def remote(source, target, send, recv, index, other):
        return pltpu.make_async_remote_copy(
            src_ref=source,
            dst_ref=target,
            send_sem=send.at[index],
            recv_sem=recv.at[index],
            device_id=other,
            device_id_type=MESH,
        )

    def reduce_one(u):
        out = []
        for k, step in enumerate(PEERS):
            at_x, at_y = lax.rem(x + step, SIDE), lax.rem(y + step, SIDE)
            out.append(
                remote(
                    partial.at[u, at_x, :, :, first],
                    landed_one.at[u, 0, k],
                    reduce_send,
                    reduce_recv,
                    (u, 0, 0, k),
                    along_x[k],
                )
            )
            out.append(
                remote(
                    partial.at[u, :, at_y, :, second],
                    landed_one.at[u, 1, k],
                    reduce_send,
                    reduce_recv,
                    (u, 0, 1, k),
                    along_y[k],
                )
            )
        return out

    def reduce_middle(u):
        own = (partial[u, x, :, :, :half], partial[u, :, y, :, half:])
        for part in range(2):
            total = own[part].astype(F32)
            for k in range(len(PEERS)):
                total = total + landed_one[u, part, k].astype(F32)
            middle[u, part] = total.astype(BF16)

    def reduce_two(u):
        out = []
        for k, step in enumerate(PEERS):
            at_x, at_y = lax.rem(x + step, SIDE), lax.rem(y + step, SIDE)
            for part, (at, peers) in enumerate(((at_y, along_y), (at_x, along_x))):
                out.append(
                    remote(
                        middle.at[u, part, at],
                        landed_two.at[u, part, k],
                        reduce_send,
                        reduce_recv,
                        (u, 1, part, k),
                        peers[k],
                    )
                )
        return out

    def reduce_end(u):
        sums = []
        for part, at in enumerate((y, x)):
            total = middle[u, part, at].astype(F32)
            for k in range(len(PEERS)):
                total = total + landed_two[u, part, k].astype(F32)
            sums.append(total)
        return jnp.concatenate(sums, axis=-1)

    sent = []

    def start(copies):
        for copy in copies:
            copy.start()
        sent.extend(copies)
        return copies

    def arrive(copies):
        for copy in copies:
            copy.wait_recv()

    own_tokens = lax.broadcasted_iota(jnp.int32, (tokens, 1), 0)
    col = own_tokens // (SIDE * rows)
    row = lax.rem(own_tokens // rows, SIDE)
    wanted = ((row * SIDE + col) * CORES + core) * rows + lax.rem(own_tokens, rows)

    def factor(routes, gates, step):
        chosen = jnp.where(routes[step] == y, gates[step], 0.0)
        line = jnp.sum(chosen, axis=0, keepdims=True)
        lanes = lax.broadcasted_iota(jnp.int32, (tokens, line.shape[-1]), 1)
        return jnp.sum(jnp.where(lanes == wanted, line, 0.0), axis=-1, keepdims=True)

    def tile_of(u, columns):
        return gathered[u, :, :, :, columns].reshape(tokens, TILE)

    tiles = width // TILE

    def pre_activation(u):
        def body(i, total):
            columns = pl.ds(pl.multiple_of(i * TILE, TILE), TILE)
            return total + jnp.dot(
                tile_of(u, columns), w_in[columns, :], preferred_element_type=F32
            )

        return lax.fori_loop(0, tiles, body, jnp.zeros((tokens, 4 * unit), F32))

    def forward(u, target, factor_column):
        both = pre_activation(u)
        a, up = both[:, : 2 * unit], both[:, 2 * unit :]
        hidden = (a / (1.0 + jnp.exp(-a)) * up).astype(BF16)

        @pl.loop(0, tiles)
        def _(i):
            columns = pl.ds(pl.multiple_of(i * TILE, TILE), TILE)
            piece = jnp.dot(hidden, w_back[:, columns], preferred_element_type=F32)
            partial[target, :, :, :, columns] = (
                (piece * factor_column).astype(BF16).reshape(SIDE, SIDE, rows, TILE)
            )

    contract = (((1,), (1,)), ((), ()))

    def backward(u, target, both, factor_column):
        a, up = both[:, : 2 * unit], both[:, 2 * unit :]

        def body(i, total):
            columns = pl.ds(pl.multiple_of(i * TILE, TILE), TILE)
            return total + lax.dot_general(
                tile_of(u, columns), w_back[:, columns], contract, preferred_element_type=F32
            )

        d_hidden = lax.fori_loop(0, tiles, body, jnp.zeros((tokens, 2 * unit), F32))
        d_hidden = d_hidden * factor_column
        sigma = 1.0 / (1.0 + jnp.exp(-a))
        d_gate = (d_hidden * up * sigma * (1.0 + a * (1.0 - sigma))).astype(BF16)
        d_up = (d_hidden * a * sigma).astype(BF16)
        grads = jnp.concatenate([d_gate, d_up], axis=-1)

        @pl.loop(0, tiles)
        def _(i):
            columns = pl.ds(pl.multiple_of(i * TILE, TILE), TILE)
            piece = lax.dot_general(
                grads, w_in[columns, :], contract, preferred_element_type=F32
            )
            partial[target, :, :, :, columns] = piece.astype(BF16).reshape(
                SIDE, SIDE, rows, TILE
            )

    def forward_end(u, inputs):
        return (inputs.astype(F32) + reduce_end(u)).astype(BF16)

    def backward_end(u, step, upstream):
        inputs = in_s[step].astype(F32)
        scale = scales[step]
        product = reduce_end(u) * gain_row
        change = scale * product - inputs * scale**3 * jnp.mean(
            product * inputs, axis=-1, keepdims=True
        )
        return (upstream.astype(F32) + change).astype(BF16)

    gather_f = start(gather_one(0))
    weights = []
    for i, (source, target) in enumerate(sibling_weights):
        weights.append(
            pltpu.make_async_remote_copy(
                src_ref=source,
                dst_ref=target,
                send_sem=weight_send.at[i],
                recv_sem=weight_recv.at[i],
                device_id=sibling,
                device_id_type=MESH,
            )
        )
    start(weights)
    gather_s = start(gather_one(1))
    gather_g = start(gather_one(2))
    factors_f = [factor(routes_f, gates_f, step) for step in range(2)]
    factors_b = [factor(routes_b, gates_b, step) for step in range(2)]
    arrive(gather_f)
    gather_f = start(gather_two(0))
    arrive(gather_s)
    gather_s = start(gather_two(1))
    arrive(gather_g)
    gather_g = start(gather_two(2))
    for load in loads[len(small) :]:
        load.wait()
    arrive(weights)
    arrive(gather_f)
    forward(0, 0, factors_f[0])
    reduce_f = start(reduce_one(0))
    arrive(gather_s)
    both = pre_activation(1)
    arrive(gather_g)
    backward(2, 1, both, factors_b[0])
    reduce_b = start(reduce_one(1))
    gather_s = start(gather_one(4))
    arrive(reduce_f)
    reduce_middle(0)
    reduce_f = start(reduce_two(0))
    arrive(reduce_b)
    reduce_middle(1)
    reduce_b = start(reduce_two(1))
    arrive(gather_s)
    gather_s = start(gather_two(4))
    arrive(reduce_f)
    outputs = forward_end(0, in_f[...])
    hop_send[0] = outputs
    hop_f = start([remote(hop_send.at[0], hop_land.at[0], hop_send_sem, hop_recv_sem, (0,), following)])
    fwd_out[0, 0] = outputs
    arrive(reduce_b)
    outputs = backward_end(1, 0, in_b[...])
    hop_send[1] = outputs
    hop_b = start([remote(hop_send.at[1], hop_land.at[1], hop_send_sem, hop_recv_sem, (1,), preceding)])
    bwd_out[0, 0] = outputs

    arrive(hop_f)
    moved_f = jnp.where(section == 0, enter_f[...].astype(F32), hop_land[0].astype(F32))
    _, normed = normalize(moved_f, gain_row)
    gathered[3, x, y] = normed
    gather_f = start(gather_one(3))
    arrive(hop_b)
    moved_b = jnp.where(
        section == sections - 1, enter_b[...].astype(F32), hop_land[1].astype(F32)
    ).astype(BF16)
    gathered[5, x, y] = moved_b
    gather_g = start(gather_one(5))
    arrive(gather_s)
    pre_act[...] = pre_activation(4)
    arrive(gather_f)
    gather_f = start(gather_two(3))
    arrive(gather_g)
    gather_g = start(gather_two(5))
    arrive(gather_f)
    forward(3, 2, factors_f[1])
    reduce_f = start(reduce_one(2))
    arrive(gather_g)
    backward(5, 3, pre_act[...], factors_b[1])
    reduce_b = start(reduce_one(3))
    arrive(reduce_f)
    reduce_middle(2)
    reduce_f = start(reduce_two(2))
    arrive(reduce_b)
    reduce_middle(3)
    reduce_b = start(reduce_two(3))
    arrive(reduce_f)
    fwd_out[0, 1] = forward_end(2, moved_f)
    arrive(reduce_b)
    bwd_out[0, 1] = backward_end(3, 1, moved_b)
    for copy in sent:
        copy.wait_send()


def per_device(
    fwd_in,
    fwd_enter,
    bwd_in,
    bwd_enter,
    saved,
    fwd_routes,
    fwd_gates,
    bwd_routes,
    bwd_gates,
    gain,
    w_gate,
    w_up,
    w_down,
):
    sections = lax.axis_size("section")
    steps, rows, width = saved.shape[1:]
    unit = w_gate.shape[-1]
    half = width // 2
    peers = len(PEERS)
    turned = [
        jnp.transpose(array[0], (0, 2, 1)) for array in (fwd_routes, fwd_gates, bwd_routes, bwd_gates)
    ]
    in_hbm = pl.BlockSpec(memory_space=pltpu.HBM)
    in_vmem = pl.BlockSpec(memory_space=pltpu.VMEM)
    table = turned[0].shape
    dma = pltpu.SemaphoreType.DMA
    scratch = [
        pltpu.VMEM((rows, width), BF16),
        pltpu.VMEM((rows, width), BF16),
        pltpu.VMEM((rows, width), BF16),
        pltpu.VMEM((rows, width), BF16),
        pltpu.VMEM((steps, rows, width), BF16),
        pltpu.VMEM(table, jnp.int32),
        pltpu.VMEM(table, F32),
        pltpu.VMEM(table, jnp.int32),
        pltpu.VMEM(table, F32),
        pltpu.VMEM((1, width), F32),
        pltpu.VMEM((width, 4 * unit), BF16),
        pltpu.VMEM((2 * unit, width), BF16),
        pltpu.VMEM((6, SIDE, SIDE, rows, width), BF16),
        pltpu.VMEM((4, SIDE, SIDE, rows, width), BF16),
        pltpu.VMEM((4, 2, peers, SIDE, rows, half), BF16),
        pltpu.VMEM((4, 2, SIDE, rows, half), BF16),
        pltpu.VMEM((4, 2, peers, rows, half), BF16),
        pltpu.VMEM((2, rows, width), BF16),
        pltpu.VMEM((2, rows, width), BF16),
        pltpu.VMEM((SIDE * SIDE * rows, 4 * unit), F32),
        dma((13,)),
        dma((3,)),
        dma((3,)),
        dma((6, 2, 2, peers)),
        dma((6, 2, 2, peers)),
        dma((4, 2, 2, peers)),
        dma((4, 2, 2, peers)),
        dma((2,)),
        dma((2,)),
    ]
    out = jax.ShapeDtypeStruct((1, steps, rows, width), BF16)
    return pl.pallas_call(
        functools.partial(relay_kernel, sections),
        out_shape=(out, out),
        in_specs=[in_hbm] * 13,
        out_specs=(in_vmem, in_vmem),
        scratch_shapes=scratch,
        compiler_params=pltpu.CompilerParams(
            collective_id=0, has_side_effects=True, vmem_limit_bytes=60 * 2**20
        ),
        name="relay",
    )(
        fwd_in,
        fwd_enter,
        bwd_in,
        bwd_enter,
        saved,
        *turned,
        gain,
        w_gate[0],
        w_up[0],
        w_down[0],
    )


def solution(mesh):
    in_specs = (
        P("section", "expert", None),
        P(None, "expert", None),
        P("section", "expert", None),
        P(None, "expert", None),
        P("section", None, "expert", None),
        P("section", None, None, None),
        P("section", None, None, None),
        P("section", None, None, None),
        P("section", None, None, None),
        P("section", None),
        P("section", None, "expert"),
        P("section", None, "expert"),
        P("section", "expert", None),
    )
    out_specs = (P("section", None, "expert", None), P("section", None, "expert", None))
    return jax.shard_map(
        per_device, mesh=mesh, in_specs=in_specs, out_specs=out_specs, check_vma=False
    )
```

time: 339 us -> 89.7 us (0.26)
  the two profiles are of different devices: /device:TPU:1 before, /device:TPU:2 now
where the time goes in v1:
time: 89.7 us; the launch traced here: 89.5 us
  Pallas kernels  86.7 us (97%)
  local copies, waits for them, and re-layouts  2.24 us (2%)
    pallas_call x1, Pallas kernels, per_device(): pl.pallas_call(functools.partial(relay_kernel, sections), out_shape=(out,...  86.7 us
    unnamed x4, local copies, waits for them, and re-layouts  2.24 us

profile of v1, /device:TPU:2, one launch (start us, length us, event | category | flops | bytes accessed | tf_op | source)
XLA Modules:
  0.0 89.5 jit_solution(2718597961637259329)
XLA Ops:
  0.6 86.7 %relay.1 = (bf16[1,2,8,3584]{3,2,1,0:T(8,128)(2,1)}, bf16[1,2,8,3584]{3,2,1,0:T(8,128)(2,1)}) custom-call(bf16[1,8,3584]{2,1,0:T(8,128)(2,1)} %fwd_in.1, bf16[1,8,3584]{2,1,0:T(8,128)(2,1)} %fwd_enter.1, bf16[1,8,3584]{2,1,0:T(8,128)(2,1)} %bwd_in.1, bf16[1,8,3584]{2,1,0:T(8,128)(2,1)} %bwd_enter.1, bf16[1,2,8,3584]{3,2,1,0:T(8,128)(2,1)} %saved.1, ...), custom_call_target="tpu_custom_call" | custom-call | tf_op jit(solution)/shard_map/relay/pallas_call | solution.py:472
  87.3 0.0 copy-start
  87.3 1.6 %copy.17 = bf16[1,2,8,3584]{3,2,1,0:T(8,128)(2,1)} copy(bf16[1,2,8,3584]{3,2,1,0:T(8,128)(2,1)} %get-tuple-element.4) | data formatting | bytes 229376
  88.9 0.0 copy-done
  88.9 0.6 copy.18
Async XLA Ops:
  87.3 1.6 %copy-start = (bf16[1,2,8,3584]{3,2,1,0:T(8,128)(2,1)S(1)}, bf16[1,2,8,3584]{3,2,1,0:T(8,128)(2,1)}, u32[]{:S(2)}) copy-start(bf16[1,2,8,3584]{3,2,1,0:T(8,128)(2,1)} %get-tuple-element.5) | copy-start | bytes 344068

commit v2 on v1

v2 whole, which is shorter than its diff:
```python
import functools

import jax
import jax.numpy as jnp
from jax import lax
from jax.experimental import pallas as pl
from jax.experimental.pallas import tpu as pltpu
from jax.sharding import PartitionSpec as P

EPSILON = 1e-06
MESH = pl.DeviceIdType.MESH
SIDE = 4
CORES = 2
PEERS = (1, 2, 3)
CAP = 6
F32 = jnp.float32
BF16 = jnp.bfloat16


def normalize(inputs, gain):
    scale = lax.rsqrt(jnp.mean(inputs * inputs, axis=-1, keepdims=True) + EPSILON)
    return scale, (inputs * scale * gain).astype(BF16)


def relay_kernel(
    sections,
    fwd_in,
    fwd_enter,
    bwd_in,
    bwd_enter,
    saved,
    fwd_routes,
    fwd_gates,
    bwd_routes,
    bwd_gates,
    gain,
    w_gate,
    w_up,
    w_down,
    fwd_out,
    bwd_out,
    in_f,
    enter_f,
    in_b,
    enter_b,
    in_s,
    routes_f,
    gates_f,
    routes_b,
    gates_b,
    gain_v,
    w_in,
    w_back,
    line_y,
    line_x,
    packed_x,
    packed_y,
    outgoing,
    partial_x,
    partial_y,
    landed_x,
    landed_y,
    middle,
    landed_two,
    hop_send,
    hop_land,
    pre_act,
    pick_x,
    pick_y,
    weight_of,
    load_sem,
    weight_send,
    weight_recv,
    gather_send,
    gather_recv,
    reduce_send,
    reduce_recv,
    hop_send_sem,
    hop_recv_sem,
):
    width = gain.shape[-1]
    half = width // 2
    unit = w_down.shape[0]
    rows = in_f.shape[0]
    tokens = SIDE * SIDE * rows
    section = lax.axis_index("section")
    place = lax.axis_index("expert")
    core = lax.rem(place, CORES)
    x = lax.rem(place // CORES, SIDE)
    y = place // (CORES * SIDE)

    def device(dy=0, dx=0, dc=0, dz=0):
        at_y, at_x = lax.rem(y + dy, SIDE), lax.rem(x + dx, SIDE)
        at_c = lax.rem(core + dc, CORES)
        return (lax.rem(section + dz, sections), (at_y * SIDE + at_x) * CORES + at_c)

    sibling = device(dc=1)
    following, preceding = device(dz=1), device(dz=sections - 1)
    along_y = [device(dy=k) for k in PEERS]
    along_x = [device(dx=k) for k in PEERS]

    barrier = pltpu.get_barrier_semaphore()
    greeted = [sibling, following, preceding] + along_y + along_x
    for other in greeted:
        pl.semaphore_signal(barrier, inc=1, device_id=other, device_id_type=MESH)

    small = [
        (fwd_in.at[0], in_f),
        (gain, gain_v),
        (saved.at[0], in_s),
        (bwd_in.at[0], in_b),
        (fwd_routes, routes_f),
        (fwd_gates, gates_f),
        (bwd_routes, routes_b),
        (bwd_gates, gates_b),
        (fwd_enter.at[0], enter_f),
        (bwd_enter.at[0], enter_b),
    ]
    own_weights = [
        (w_gate, w_in.at[:, pl.ds(0, unit)]),
        (w_up, w_in.at[:, pl.ds(2 * unit, unit)]),
        (w_down, w_back.at[pl.ds(0, unit), :]),
    ]
    sibling_weights = [
        (w_gate, w_in.at[:, pl.ds(unit, unit)]),
        (w_up, w_in.at[:, pl.ds(3 * unit, unit)]),
        (w_down, w_back.at[pl.ds(unit, unit), :]),
    ]
    loads = [
        pltpu.make_async_copy(source, target, load_sem.at[i])
        for i, (source, target) in enumerate(small + own_weights)
    ]
    for load in loads:
        load.start()
    for load in loads[: len(small)]:
        load.wait()

    gain_row = gain_v[...]
    first, second = pl.ds(0, half), pl.ds(half, half)

    def place_own(u, block):
        line_y[u, y] = block[:, :half]
        line_x[u, x] = block[:, half:]

    _, normed = normalize(in_f[...].astype(F32), gain_row)
    place_own(0, normed)
    scales = []
    for step in range(2):
        scale, normed = normalize(in_s[step].astype(F32), gain_row)
        scales.append(scale)
        place_own(1 + 3 * step, normed)
    place_own(2, in_b[...])

    pl.semaphore_wait(barrier, len(greeted))

    sent = []

    def start(copies):
        for copy in copies:
            copy.start()
        sent.extend(copies)
        return copies

    def arrive(copies):
        for copy in copies:
            copy.wait_recv()

    def remote(source, target, send, recv, index, other):
        return pltpu.make_async_remote_copy(
            src_ref=source,
            dst_ref=target,
            send_sem=send.at[index],
            recv_sem=recv.at[index],
            device_id=other,
            device_id_type=MESH,
        )

    blocks = SIDE * SIDE * CORES
    slots = SIDE * CAP
    whole = SIDE * slots

    def iota(shape, axis):
        return lax.broadcasted_iota(jnp.int32, shape, axis)

    def choose():
        experts = iota((SIDE, blocks * rows), 0)
        hits, lines = [], []
        for routes, gates in ((routes_f, gates_f), (routes_b, gates_b)):
            for step in range(2):
                chosen = [routes[step, k : k + 1] == experts for k in range(2)]
                hits.append(jnp.where(chosen[0] | chosen[1], 1.0, 0.0))
                own = [jnp.where(routes[step, k : k + 1] == y, gates[step, k : k + 1], 0.0) for k in range(2)]
                lines.append(own[0] + own[1])
        hit = jnp.concatenate(hits, axis=0)
        from_lane, to_lane = (iota((blocks * rows, blocks * rows), axis) for axis in (0, 1))
        earlier = (from_lane // rows == to_lane // rows) & (from_lane < to_lane)
        rank = jnp.dot(
            hit.astype(BF16), jnp.where(earlier, 1.0, 0.0).astype(BF16), preferred_element_type=F32
        )
        key = jnp.where(hit > 0.5, rank, 64.0)
        lane, spot = iota((blocks * rows, SIDE * rows), 0), iota((blocks * rows, SIDE * rows), 1)
        near = lax.rem(spot, rows)
        in_column = lane == (((spot // rows) * SIDE + x) * CORES + core) * rows + near
        in_row = lane == ((y * SIDE + spot // rows) * CORES + core) * rows + near
        keys = [
            jnp.dot(
                key.astype(BF16), jnp.where(at, 1.0, 0.0).astype(BF16), preferred_element_type=F32
            )
            for at in (in_column, in_row)
        ]
        slot, spot = iota((slots, SIDE * rows), 0), iota((slots, SIDE * rows), 1)
        aligned = spot // rows == slot // CAP
        number = lax.rem(slot, CAP).astype(F32)
        order = iota((whole, blocks * rows), 0)
        lanes = iota((whole, blocks * rows), 1)
        block = (lax.rem(order // CAP, SIDE) * SIDE + order // slots) * CORES + core
        mine = lanes // rows == block
        position = lax.rem(order, CAP).astype(F32)
        is_own = iota((SIDE, SIDE * rows), 0) == y
        is_own_wide = iota((SIDE, blocks * rows), 0) == y
        for r in range(4):
            part = slice(r * SIDE, (r + 1) * SIDE)
            own = jnp.sum(jnp.where(is_own, keys[0][part], 0.0), axis=0, keepdims=True)
            pick_x[r] = jnp.where(aligned & (own == number), 1.0, 0.0)
            for e in range(SIDE):
                here = keys[1][r * SIDE + e : r * SIDE + e + 1]
                pick_y[r, e * slots : (e + 1) * slots] = jnp.where(
                    aligned & (here == number), 1.0, 0.0
                )
            own = jnp.sum(jnp.where(is_own_wide, key[part], 0.0), axis=0, keepdims=True)
            weight_of[r] = jnp.sum(
                jnp.where(mine & (own == position), lines[r], 0.0), axis=-1, keepdims=True
            )

    order, other = iota((whole, whole), 0), iota((whole, whole), 1)
    turned = lax.rem(order // CAP, SIDE) * slots + (order // slots) * CAP + lax.rem(order, CAP)
    turn = jnp.where(turned == other, 1.0, 0.0).astype(BF16)

    def gather_one(u):
        out = []
        for k in range(len(PEERS)):
            spot = line_y.at[u, y]
            out.append(remote(spot, spot, gather_send, gather_recv, (u, 0, 0, k), along_y[k]))
            spot = line_x.at[u, x]
            out.append(remote(spot, spot, gather_send, gather_recv, (u, 0, 1, k), along_x[k]))
        return out

    tiles = slots // rows

    def gather_two(u, r):
        out = []
        block = line_y[u].reshape(SIDE * rows, half)
        packed = jnp.dot(pick_x[r].astype(BF16), block, preferred_element_type=F32)
        packed_x[u, x] = packed.astype(BF16).reshape(tiles, rows, half)
        for k in range(len(PEERS)):
            spot = packed_x.at[u, x]
            out.append(remote(spot, spot, gather_send, gather_recv, (u, 1, 0, k), along_x[k]))
        block = line_x[u].reshape(SIDE * rows, half)
        packed = jnp.dot(pick_y[r].astype(BF16), block, preferred_element_type=F32)
        outgoing[u] = packed.astype(BF16).reshape(SIDE, tiles, rows, half)
        for k, step in enumerate(PEERS):
            source, target = outgoing.at[u, lax.rem(y + step, SIDE)], packed_y.at[u, y]
            out.append(remote(source, target, gather_send, gather_recv, (u, 1, 1, k), along_y[k]))
        packed_y[u, y] = outgoing[u, y]
        return out

    def halves(u):
        by_row = jnp.dot(turn, packed_y[u].reshape(whole, half), preferred_element_type=F32)
        return packed_x[u].reshape(whole, half), by_row.astype(BF16)

    def reduce_one(u):
        out = []
        for k, step in enumerate(PEERS):
            source, target = partial_x.at[u, lax.rem(x + step, SIDE)], landed_x.at[u, k]
            out.append(remote(source, target, reduce_send, reduce_recv, (u, 0, 0, k), along_x[k]))
            source, target = partial_y.at[u, lax.rem(y + step, SIDE)], landed_y.at[u, y]
            out.append(remote(source, target, reduce_send, reduce_recv, (u, 0, 1, k), along_y[k]))
        landed_y[u, y] = partial_y[u, y]
        return out

    transposed = (((0,), (0,)), ((), ()))

    def reduce_two(u, r):
        total = partial_x[u, x].astype(F32)
        for k in range(len(PEERS)):
            total = total + landed_x[u, k].astype(F32)
        spread = lax.dot_general(
            pick_x[r].astype(BF16),
            total.astype(BF16).reshape(slots, half),
            transposed,
            preferred_element_type=F32,
        )
        middle[u, 0] = spread.astype(BF16).reshape(SIDE, rows, half)
        spread = lax.dot_general(
            pick_y[r].astype(BF16),
            landed_y[u].reshape(whole, half),
            transposed,
            preferred_element_type=F32,
        )
        middle[u, 1] = spread.astype(BF16).reshape(SIDE, rows, half)
        out = []
        for k, step in enumerate(PEERS):
            at_x, at_y = lax.rem(x + step, SIDE), lax.rem(y + step, SIDE)
            for part, (at, peers) in enumerate(((at_y, along_y), (at_x, along_x))):
                source, target = middle.at[u, part, at], landed_two.at[u, part, k]
                index = (u, 1, part, k)
                out.append(remote(source, target, reduce_send, reduce_recv, index, peers[k]))
        return out

    def reduce_end(u):
        sums = []
        for part, at in enumerate((y, x)):
            total = middle[u, part, at].astype(F32)
            for k in range(len(PEERS)):
                total = total + landed_two[u, part, k].astype(F32)
            sums.append(total)
        return jnp.concatenate(sums, axis=-1)

    def pre_activation(u):
        by_column, by_row = halves(u)
        both = jnp.dot(by_column, w_in[first, :], preferred_element_type=F32)
        return both + jnp.dot(by_row, w_in[second, :], preferred_element_type=F32)

    shape = (SIDE, tiles, rows, half)

    def turn_rows(array):
        return jnp.dot(turn, array, preferred_element_type=F32).astype(BF16)

    def forward(u, target, r):
        both = pre_activation(u)
        a, up = both[:, : 2 * unit], both[:, 2 * unit :]
        hidden = (a / (1.0 + jnp.exp(-a)) * up * weight_of[r]).astype(BF16)
        piece = jnp.dot(hidden, w_back[:, first], preferred_element_type=F32)
        partial_x[target] = piece.astype(BF16).reshape(shape)
        piece = jnp.dot(turn_rows(hidden), w_back[:, second], preferred_element_type=F32)
        partial_y[target] = piece.astype(BF16).reshape(shape)

    contract = (((1,), (1,)), ((), ()))

    def backward(u, target, both, r):
        a, up = both[:, : 2 * unit], both[:, 2 * unit :]
        by_column, by_row = halves(u)
        d_hidden = lax.dot_general(
            by_column, w_back[:, first], contract, preferred_element_type=F32
        ) + lax.dot_general(by_row, w_back[:, second], contract, preferred_element_type=F32)
        d_hidden = d_hidden * weight_of[r]
        sigma = 1.0 / (1.0 + jnp.exp(-a))
        d_gate = (d_hidden * up * sigma * (1.0 + a * (1.0 - sigma))).astype(BF16)
        d_up = (d_hidden * a * sigma).astype(BF16)
        grads = jnp.concatenate([d_gate, d_up], axis=-1)
        piece = lax.dot_general(grads, w_in[first, :], contract, preferred_element_type=F32)
        partial_x[target] = piece.astype(BF16).reshape(shape)
        piece = lax.dot_general(
            turn_rows(grads), w_in[second, :], contract, preferred_element_type=F32
        )
        partial_y[target] = piece.astype(BF16).reshape(shape)

    def forward_end(u, inputs):
        return (inputs.astype(F32) + reduce_end(u)).astype(BF16)

    def backward_end(u, step, upstream):
        inputs = in_s[step].astype(F32)
        scale = scales[step]
        product = reduce_end(u) * gain_row
        change = scale * product - inputs * scale**3 * jnp.mean(
            product * inputs, axis=-1, keepdims=True
        )
        return (upstream.astype(F32) + change).astype(BF16)

    def hop(i, block, other):
        hop_send[i] = block
        return start(
            [remote(hop_send.at[i], hop_land.at[i], hop_send_sem, hop_recv_sem, (i,), other)]
        )

    gather_f = start(gather_one(0))
    weights = [
        remote(source, target, weight_send, weight_recv, (i,), sibling)
        for i, (source, target) in enumerate(sibling_weights)
    ]
    start(weights)
    gather_s = start(gather_one(1))
    gather_g = start(gather_one(2))
    choose()
    arrive(gather_f)
    gather_f = start(gather_two(0, 0))
    arrive(gather_s)
    gather_s = start(gather_two(1, 2))
    arrive(gather_g)
    gather_g = start(gather_two(2, 2))
    for load in loads[len(small) :]:
        load.wait()
    arrive(weights)
    arrive(gather_f)
    forward(0, 0, 0)
    reduce_f = start(reduce_one(0))
    gather_n = start(gather_one(4))
    arrive(gather_s)
    both = pre_activation(1)
    arrive(gather_g)
    backward(2, 1, both, 2)
    reduce_b = start(reduce_one(1))
    arrive(reduce_f)
    reduce_f = start(reduce_two(0, 0))
    arrive(gather_n)
    gather_n = start(gather_two(4, 3))
    arrive(reduce_b)
    reduce_b = start(reduce_two(1, 2))
    arrive(reduce_f)
    outputs = forward_end(0, in_f[...])
    hop_f = hop(0, outputs, following)
    fwd_out[0, 0] = outputs
    arrive(reduce_b)
    outputs = backward_end(1, 0, in_b[...])
    hop_b = hop(1, outputs, preceding)
    bwd_out[0, 0] = outputs

    arrive(hop_f)
    moved_f = jnp.where(section == 0, enter_f[...].astype(F32), hop_land[0].astype(F32))
    _, normed = normalize(moved_f, gain_row)
    place_own(3, normed)
    gather_f = start(gather_one(3))
    arrive(hop_b)
    moved_b = jnp.where(
        section == sections - 1, enter_b[...].astype(F32), hop_land[1].astype(F32)
    ).astype(BF16)
    place_own(5, moved_b)
    gather_g = start(gather_one(5))
    arrive(gather_n)
    pre_act[...] = pre_activation(4)
    arrive(gather_f)
    gather_f = start(gather_two(3, 1))
    arrive(gather_g)
    gather_g = start(gather_two(5, 3))
    arrive(gather_f)
    forward(3, 2, 1)
    reduce_f = start(reduce_one(2))
    arrive(gather_g)
    backward(5, 3, pre_act[...], 3)
    reduce_b = start(reduce_one(3))
    arrive(reduce_f)
    reduce_f = start(reduce_two(2, 1))
    arrive(reduce_b)
    reduce_b = start(reduce_two(3, 3))
    arrive(reduce_f)
    fwd_out[0, 1] = forward_end(2, moved_f)
    arrive(reduce_b)
    bwd_out[0, 1] = backward_end(3, 1, moved_b)
    for copy in sent:
        copy.wait_send()


def per_device(
    fwd_in,
    fwd_enter,
    bwd_in,
    bwd_enter,
    saved,
    fwd_routes,
    fwd_gates,
    bwd_routes,
    bwd_gates,
    gain,
    w_gate,
    w_up,
    w_down,
):
    sections = lax.axis_size("section")
    steps, rows, width = saved.shape[1:]
    unit = w_gate.shape[-1]
    half = width // 2
    peers = len(PEERS)
    tiles = SIDE * CAP // rows
    turned = [
        jnp.transpose(array[0], (0, 2, 1)) for array in (fwd_routes, fwd_gates, bwd_routes, bwd_gates)
    ]
    in_hbm = pl.BlockSpec(memory_space=pltpu.HBM)
    in_vmem = pl.BlockSpec(memory_space=pltpu.VMEM)
    table = turned[0].shape
    dma = pltpu.SemaphoreType.DMA
    scratch = [
        pltpu.VMEM((rows, width), BF16),
        pltpu.VMEM((rows, width), BF16),
        pltpu.VMEM((rows, width), BF16),
        pltpu.VMEM((rows, width), BF16),
        pltpu.VMEM((steps, rows, width), BF16),
        pltpu.VMEM(table, jnp.int32),
        pltpu.VMEM(table, F32),
        pltpu.VMEM(table, jnp.int32),
        pltpu.VMEM(table, F32),
        pltpu.VMEM((1, width), F32),
        pltpu.VMEM((width, 4 * unit), BF16),
        pltpu.VMEM((2 * unit, width), BF16),
        pltpu.VMEM((6, SIDE, rows, half), BF16),
        pltpu.VMEM((6, SIDE, rows, half), BF16),
        pltpu.VMEM((6, SIDE, tiles, rows, half), BF16),
        pltpu.VMEM((6, SIDE, tiles, rows, half), BF16),
        pltpu.VMEM((6, SIDE, tiles, rows, half), BF16),
        pltpu.VMEM((4, SIDE, tiles, rows, half), BF16),
        pltpu.VMEM((4, SIDE, tiles, rows, half), BF16),
        pltpu.VMEM((4, peers, tiles, rows, half), BF16),
        pltpu.VMEM((4, SIDE, tiles, rows, half), BF16),
        pltpu.VMEM((4, 2, SIDE, rows, half), BF16),
        pltpu.VMEM((4, 2, peers, rows, half), BF16),
        pltpu.VMEM((2, rows, width), BF16),
        pltpu.VMEM((2, rows, width), BF16),
        pltpu.VMEM((SIDE * SIDE * CAP, 4 * unit), F32),
        pltpu.VMEM((4, SIDE * CAP, SIDE * rows), F32),
        pltpu.VMEM((4, SIDE * SIDE * CAP, SIDE * rows), F32),
        pltpu.VMEM((4, SIDE * SIDE * CAP, 1), F32),
        dma((13,)),
        dma((3,)),
        dma((3,)),
        dma((6, 2, 2, peers)),
        dma((6, 2, 2, peers)),
        dma((4, 2, 2, peers)),
        dma((4, 2, 2, peers)),
        dma((2,)),
        dma((2,)),
    ]
    out = jax.ShapeDtypeStruct((1, steps, rows, width), BF16)
    return pl.pallas_call(
        functools.partial(relay_kernel, sections),
        out_shape=(out, out),
        in_specs=[in_hbm] * 13,
        out_specs=(in_vmem, in_vmem),
        scratch_shapes=scratch,
        compiler_params=pltpu.CompilerParams(
            collective_id=0, has_side_effects=True, vmem_limit_bytes=60 * 2**20
        ),
        name="relay",
    )(
        fwd_in,
        fwd_enter,
        bwd_in,
        bwd_enter,
        saved,
        *turned,
        gain,
        w_gate[0],
        w_up[0],
        w_down[0],
    )


def solution(mesh):
    in_specs = (
        P("section", "expert", None),
        P(None, "expert", None),
        P("section", "expert", None),
        P(None, "expert", None),
        P("section", None, "expert", None),
        P("section", None, None, None),
        P("section", None, None, None),
        P("section", None, None, None),
        P("section", None, None, None),
        P("section", None),
        P("section", None, "expert"),
        P("section", None, "expert"),
        P("section", "expert", None),
    )
    out_specs = (P("section", None, "expert", None), P("section", None, "expert", None))
    return jax.shard_map(
        per_device, mesh=mesh, in_specs=in_specs, out_specs=out_specs, check_vma=False
    )
```

time: 89.7 us -> 79.3 us (0.88)
  Pallas kernels: 86.7 us -> 76.2 us
    pallas_call x1, Pallas kernels: 86.7 us -> 76.2 us  [per_device(): pl.pallas_call(functools.partial(relay_kernel, sections), out_shape=(out,...]
where the time goes in v2:
time: 79.3 us; the launch traced here: 79.1 us
  Pallas kernels  76.2 us (96%)
  local copies, waits for them, and re-layouts  2.24 us (3%)
    pallas_call x1, Pallas kernels, per_device(): pl.pallas_call(functools.partial(relay_kernel, sections), out_shape=(out,...  76.2 us
    unnamed x4, local copies, waits for them, and re-layouts  2.24 us

profile of v2, /device:TPU:2, one launch (start us, length us, event | category | flops | bytes accessed | tf_op | source)
XLA Modules:
  0.0 79.1 jit_solution(18145469128212557788)
XLA Ops:
  0.6 76.2 %relay.1 = (bf16[1,2,8,3584]{3,2,1,0:T(8,128)(2,1)}, bf16[1,2,8,3584]{3,2,1,0:T(8,128)(2,1)}) custom-call(bf16[1,8,3584]{2,1,0:T(8,128)(2,1)} %fwd_in.1, bf16[1,8,3584]{2,1,0:T(8,128)(2,1)} %fwd_enter.1, bf16[1,8,3584]{2,1,0:T(8,128)(2,1)} %bwd_in.1, bf16[1,8,3584]{2,1,0:T(8,128)(2,1)} %bwd_enter.1, bf16[1,2,8,3584]{3,2,1,0:T(8,128)(2,1)} %saved.1, ...), custom_call_target="tpu_custom_call" | custom-call | tf_op jit(solution)/shard_map/relay/pallas_call | solution.py:522
  76.9 0.0 copy-start
  76.9 1.6 %copy.17 = bf16[1,2,8,3584]{3,2,1,0:T(8,128)(2,1)} copy(bf16[1,2,8,3584]{3,2,1,0:T(8,128)(2,1)} %get-tuple-element.4) | data formatting | bytes 229376
  78.5 0.0 copy-done
  78.5 0.6 copy.18
Async XLA Ops:
  76.9 1.6 %copy-start = (bf16[1,2,8,3584]{3,2,1,0:T(8,128)(2,1)S(1)}, bf16[1,2,8,3584]{3,2,1,0:T(8,128)(2,1)}, u32[]{:S(2)}) copy-start(bf16[1,2,8,3584]{3,2,1,0:T(8,128)(2,1)} %get-tuple-element.5) | copy-start | bytes 344068

commit v3 on v2

--- a/solution.py
+++ b/solution.py
@@ -11,7 +11,7 @@
 MESH = pl.DeviceIdType.MESH
 SIDE = 4
 CORES = 2
-PEERS = (1, 2, 3)
+PEERS = (2, 1, 3)
 CAP = 6
 F32 = jnp.float32
 BF16 = jnp.bfloat16
@@ -132,9 +132,8 @@
     ]
     for load in loads:
         load.start()
-    for load in loads[: len(small)]:
-        load.wait()
-
+    loads[1].wait()
+    loads[2].wait()
     gain_row = gain_v[...]
     first, second = pl.ds(0, half), pl.ds(half, half)
 
@@ -142,15 +141,9 @@
         line_y[u, y] = block[:, :half]
         line_x[u, x] = block[:, half:]
 
-    _, normed = normalize(in_f[...].astype(F32), gain_row)
-    place_own(0, normed)
-    scales = []
-    for step in range(2):
-        scale, normed = normalize(in_s[step].astype(F32), gain_row)
-        scales.append(scale)
-        place_own(1 + 3 * step, normed)
-    place_own(2, in_b[...])
-
+    scale, normed = normalize(in_s[0].astype(F32), gain_row)
+    scales = [scale]
+    place_own(1, normed)
     pl.semaphore_wait(barrier, len(greeted))
 
     sent = []
@@ -247,40 +240,68 @@
 
     tiles = slots // rows
 
-    def gather_two(u, r):
-        out = []
+    def gather_two(u, r, ones):
+        arrive(ones[0::2])
         block = line_y[u].reshape(SIDE * rows, half)
         packed = jnp.dot(pick_x[r].astype(BF16), block, preferred_element_type=F32)
         packed_x[u, x] = packed.astype(BF16).reshape(tiles, rows, half)
-        for k in range(len(PEERS)):
-            spot = packed_x.at[u, x]
-            out.append(remote(spot, spot, gather_send, gather_recv, (u, 1, 0, k), along_x[k]))
+        spot = packed_x.at[u, x]
+        across_x = start(
+            [
+                remote(spot, spot, gather_send, gather_recv, (u, 1, 0, k), along_x[k])
+                for k in range(len(PEERS))
+            ]
+        )
+        arrive(ones[1::2])
         block = line_x[u].reshape(SIDE * rows, half)
         packed = jnp.dot(pick_y[r].astype(BF16), block, preferred_element_type=F32)
         outgoing[u] = packed.astype(BF16).reshape(SIDE, tiles, rows, half)
+        across_y = []
         for k, step in enumerate(PEERS):
             source, target = outgoing.at[u, lax.rem(y + step, SIDE)], packed_y.at[u, y]
-            out.append(remote(source, target, gather_send, gather_recv, (u, 1, 1, k), along_y[k]))
+            across_y.append(
+                remote(source, target, gather_send, gather_recv, (u, 1, 1, k), along_y[k])
+            )
+        start(across_y)
         packed_y[u, y] = outgoing[u, y]
-        return out
-
-    def halves(u):
-        by_row = jnp.dot(turn, packed_y[u].reshape(whole, half), preferred_element_type=F32)
-        return packed_x[u].reshape(whole, half), by_row.astype(BF16)
-
-    def reduce_one(u):
+        return across_x, across_y
+
+    def by_column(u):
+        return packed_x[u].reshape(whole, half)
+
+    def by_row(u):
+        return turn_rows(packed_y[u].reshape(whole, half))
+
+    def turn_rows(array):
+        return jnp.dot(turn, array, preferred_element_type=F32).astype(BF16)
+
+    def reduce_x(u):
         out = []
         for k, step in enumerate(PEERS):
             source, target = partial_x.at[u, lax.rem(x + step, SIDE)], landed_x.at[u, k]
             out.append(remote(source, target, reduce_send, reduce_recv, (u, 0, 0, k), along_x[k]))
+        return start(out)
+
+    def reduce_y(u):
+        out = []
+        for k, step in enumerate(PEERS):
             source, target = partial_y.at[u, lax.rem(y + step, SIDE)], landed_y.at[u, y]
             out.append(remote(source, target, reduce_send, reduce_recv, (u, 0, 1, k), along_y[k]))
+        start(out)
         landed_y[u, y] = partial_y[u, y]
         return out
 
     transposed = (((0,), (0,)), ((), ()))
 
-    def reduce_two(u, r):
+    def last_leg(u, part, at, peers):
+        out = []
+        for k, step in enumerate(PEERS):
+            source, target = middle.at[u, part, lax.rem(at + step, SIDE)], landed_two.at[u, part, k]
+            out.append(remote(source, target, reduce_send, reduce_recv, (u, 1, part, k), peers[k]))
+        return start(out)
+
+    def reduce_two(u, r, ones):
+        arrive(ones[0])
         total = partial_x[u, x].astype(F32)
         for k in range(len(PEERS)):
             total = total + landed_x[u, k].astype(F32)
@@ -291,6 +312,8 @@
             preferred_element_type=F32,
         )
         middle[u, 0] = spread.astype(BF16).reshape(SIDE, rows, half)
+        across_y = last_leg(u, 0, y, along_y)
+        arrive(ones[1])
         spread = lax.dot_general(
             pick_y[r].astype(BF16),
             landed_y[u].reshape(whole, half),
@@ -298,14 +321,7 @@
             preferred_element_type=F32,
         )
         middle[u, 1] = spread.astype(BF16).reshape(SIDE, rows, half)
-        out = []
-        for k, step in enumerate(PEERS):
-            at_x, at_y = lax.rem(x + step, SIDE), lax.rem(y + step, SIDE)
-            for part, (at, peers) in enumerate(((at_y, along_y), (at_x, along_x))):
-                source, target = middle.at[u, part, at], landed_two.at[u, part, k]
-                index = (u, 1, part, k)
-                out.append(remote(source, target, reduce_send, reduce_recv, index, peers[k]))
-        return out
+        return across_y + last_leg(u, 1, x, along_x)
 
     def reduce_end(u):
         sums = []
@@ -316,33 +332,36 @@
             sums.append(total)
         return jnp.concatenate(sums, axis=-1)
 
-    def pre_activation(u):
-        by_column, by_row = halves(u)
-        both = jnp.dot(by_column, w_in[first, :], preferred_element_type=F32)
-        return both + jnp.dot(by_row, w_in[second, :], preferred_element_type=F32)
+    def pre_activation(u, twos):
+        arrive(twos[0])
+        both = jnp.dot(by_column(u), w_in[first, :], preferred_element_type=F32)
+        arrive(twos[1])
+        return both + jnp.dot(by_row(u), w_in[second, :], preferred_element_type=F32)
 
     shape = (SIDE, tiles, rows, half)
 
-    def turn_rows(array):
-        return jnp.dot(turn, array, preferred_element_type=F32).astype(BF16)
-
-    def forward(u, target, r):
-        both = pre_activation(u)
+    def forward(target, r, both):
         a, up = both[:, : 2 * unit], both[:, 2 * unit :]
         hidden = (a / (1.0 + jnp.exp(-a)) * up * weight_of[r]).astype(BF16)
         piece = jnp.dot(hidden, w_back[:, first], preferred_element_type=F32)
         partial_x[target] = piece.astype(BF16).reshape(shape)
+        across_x = reduce_x(target)
         piece = jnp.dot(turn_rows(hidden), w_back[:, second], preferred_element_type=F32)
         partial_y[target] = piece.astype(BF16).reshape(shape)
+        return across_x, reduce_y(target)
 
     contract = (((1,), (1,)), ((), ()))
 
-    def backward(u, target, both, r):
+    def backward(u, target, both, r, twos):
         a, up = both[:, : 2 * unit], both[:, 2 * unit :]
-        by_column, by_row = halves(u)
+        arrive(twos[0])
         d_hidden = lax.dot_general(
-            by_column, w_back[:, first], contract, preferred_element_type=F32
-        ) + lax.dot_general(by_row, w_back[:, second], contract, preferred_element_type=F32)
+            by_column(u), w_back[:, first], contract, preferred_element_type=F32
+        )
+        arrive(twos[1])
+        d_hidden = d_hidden + lax.dot_general(
+            by_row(u), w_back[:, second], contract, preferred_element_type=F32
+        )
         d_hidden = d_hidden * weight_of[r]
         sigma = 1.0 / (1.0 + jnp.exp(-a))
         d_gate = (d_hidden * up * sigma * (1.0 + a * (1.0 - sigma))).astype(BF16)
@@ -350,10 +369,12 @@
         grads = jnp.concatenate([d_gate, d_up], axis=-1)
         piece = lax.dot_general(grads, w_in[first, :], contract, preferred_element_type=F32)
         partial_x[target] = piece.astype(BF16).reshape(shape)
+        across_x = reduce_x(target)
         piece = lax.dot_general(
             turn_rows(grads), w_in[second, :], contract, preferred_element_type=F32
         )
         partial_y[target] = piece.astype(BF16).reshape(shape)
+        return across_x, reduce_y(target)
 
     def forward_end(u, inputs):
         return (inputs.astype(F32) + reduce_end(u)).astype(BF16)
@@ -373,79 +394,69 @@
             [remote(hop_send.at[i], hop_land.at[i], hop_send_sem, hop_recv_sem, (i,), other)]
         )
 
-    gather_f = start(gather_one(0))
+    for load in [loads[0]] + loads[3 : len(small)]:
+        load.wait()
+    place_own(2, in_b[...])
+    gather_s = start(gather_one(1))
+    gather_g = start(gather_one(2))
     weights = [
         remote(source, target, weight_send, weight_recv, (i,), sibling)
         for i, (source, target) in enumerate(sibling_weights)
     ]
     start(weights)
-    gather_s = start(gather_one(1))
-    gather_g = start(gather_one(2))
+    _, normed = normalize(in_f[...].astype(F32), gain_row)
+    place_own(0, normed)
+    gather_f = start(gather_one(0))
+    scale, normed = normalize(in_s[1].astype(F32), gain_row)
+    scales.append(scale)
+    place_own(4, normed)
     choose()
-    arrive(gather_f)
-    gather_f = start(gather_two(0, 0))
-    arrive(gather_s)
-    gather_s = start(gather_two(1, 2))
-    arrive(gather_g)
-    gather_g = start(gather_two(2, 2))
+    gather_s = gather_two(1, 2, gather_s)
+    gather_g = gather_two(2, 2, gather_g)
+    gather_f = gather_two(0, 0, gather_f)
     for load in loads[len(small) :]:
         load.wait()
     arrive(weights)
-    arrive(gather_f)
-    forward(0, 0, 0)
-    reduce_f = start(reduce_one(0))
+    both = pre_activation(1, gather_s)
+    reduce_b = backward(2, 1, both, 2, gather_g)
+    both = pre_activation(0, gather_f)
+    reduce_f = forward(0, 0, both)
     gather_n = start(gather_one(4))
-    arrive(gather_s)
-    both = pre_activation(1)
-    arrive(gather_g)
-    backward(2, 1, both, 2)
-    reduce_b = start(reduce_one(1))
-    arrive(reduce_f)
-    reduce_f = start(reduce_two(0, 0))
-    arrive(gather_n)
-    gather_n = start(gather_two(4, 3))
+    reduce_b = reduce_two(1, 2, reduce_b)
+    reduce_f = reduce_two(0, 0, reduce_f)
     arrive(reduce_b)
-    reduce_b = start(reduce_two(1, 2))
+    outputs = backward_end(1, 0, in_b[...])
+    hop_b = hop(1, outputs, preceding)
+    bwd_out[0, 0] = outputs
+    gather_n = gather_two(4, 3, gather_n)
     arrive(reduce_f)
     outputs = forward_end(0, in_f[...])
     hop_f = hop(0, outputs, following)
     fwd_out[0, 0] = outputs
-    arrive(reduce_b)
-    outputs = backward_end(1, 0, in_b[...])
-    hop_b = hop(1, outputs, preceding)
-    bwd_out[0, 0] = outputs
-
-    arrive(hop_f)
-    moved_f = jnp.where(section == 0, enter_f[...].astype(F32), hop_land[0].astype(F32))
-    _, normed = normalize(moved_f, gain_row)
-    place_own(3, normed)
-    gather_f = start(gather_one(3))
+
     arrive(hop_b)
     moved_b = jnp.where(
         section == sections - 1, enter_b[...].astype(F32), hop_land[1].astype(F32)
     ).astype(BF16)
     place_own(5, moved_b)
     gather_g = start(gather_one(5))
-    arrive(gather_n)
-    pre_act[...] = pre_activation(4)
-    arrive(gather_f)
-    gather_f = start(gather_two(3, 1))
-    arrive(gather_g)
-    gather_g = start(gather_two(5, 3))
-    arrive(gather_f)
-    forward(3, 2, 1)
-    reduce_f = start(reduce_one(2))
-    arrive(gather_g)
-    backward(5, 3, pre_act[...], 3)
-    reduce_b = start(reduce_one(3))
-    arrive(reduce_f)
-    reduce_f = start(reduce_two(2, 1))
+    arrive(hop_f)
+    moved_f = jnp.where(section == 0, enter_f[...].astype(F32), hop_land[0].astype(F32))
+    _, normed = normalize(moved_f, gain_row)
+    place_own(3, normed)
+    gather_f = start(gather_one(3))
+    pre_act[...] = pre_activation(4, gather_n)
+    gather_g = gather_two(5, 3, gather_g)
+    gather_f = gather_two(3, 1, gather_f)
+    reduce_b = backward(5, 3, pre_act[...], 3, gather_g)
+    both = pre_activation(3, gather_f)
+    reduce_f = forward(2, 1, both)
+    reduce_b = reduce_two(3, 3, reduce_b)
+    reduce_f = reduce_two(2, 1, reduce_f)
     arrive(reduce_b)
-    reduce_b = start(reduce_two(3, 3))
+    bwd_out[0, 1] = backward_end(3, 1, moved_b)
     arrive(reduce_f)
     fwd_out[0, 1] = forward_end(2, moved_f)
-    arrive(reduce_b)
-    bwd_out[0, 1] = backward_end(3, 1, moved_b)
     for copy in sent:
         copy.wait_send()
 
@@ -519,7 +530,7 @@
         dma((2,)),
     ]
     out = jax.ShapeDtypeStruct((1, steps, rows, width), BF16)
-    return pl.pallas_call(
+    results = pl.pallas_call(
         functools.partial(relay_kernel, sections),
         out_shape=(out, out),
         in_specs=[in_hbm] * 13,
@@ -541,6 +552,25 @@
         w_up[0],
         w_down[0],
     )
+    return pl.pallas_call(
+        store_kernel,
+        out_shape=(out, out),
+        in_specs=[pl.BlockSpec(memory_space=pltpu.VMEM)] * 2,
+        out_specs=(pl.BlockSpec(memory_space=pl.ANY),) * 2,
+        scratch_shapes=[dma((2,))],
+        name="store",
+    )(*results)
+
+
+def store_kernel(fwd, bwd, fwd_to, bwd_to, sems):
+    copies = [
+        pltpu.make_async_copy(source, target, sems.at[i])
+        for i, (source, target) in enumerate(((fwd, fwd_to), (bwd, bwd_to)))
+    ]
+    for copy in copies:
+        copy.start()
+    for copy in copies:
+        copy.wait()
 
 
 def solution(mesh):

time: 79.3 us -> 76.4 us (0.963)
  the two profiles are of different devices: /device:TPU:2 before, /device:TPU:8 now
where the time goes in v3:
time: 76.4 us; the launch traced here: 76.2 us
  Pallas kernels  75.6 us (99%)
    pallas_call x1, Pallas kernels, per_device(): pl.pallas_call(functools.partial(relay_kernel, sections), out_shape=(out,...  73.9 us
    pallas_call x1, Pallas kernels, per_device(): pl.pallas_call(store_kernel, out_shape=(out, out), in_specs=[pl.BlockSpec...  1.65 us

profile of v3, /device:TPU:8, one launch (start us, length us, event | category | flops | bytes accessed | tf_op | source)
XLA Modules:
  0.0 76.2 jit_solution(9445612904643105880)
XLA Ops:
  0.6 73.9 %relay.1 = (bf16[1,2,8,3584]{3,2,1,0:T(8,128)(2,1)}, bf16[1,2,8,3584]{3,2,1,0:T(8,128)(2,1)}) custom-call(bf16[1,8,3584]{2,1,0:T(8,128)(2,1)} %fwd_in.1, bf16[1,8,3584]{2,1,0:T(8,128)(2,1)} %fwd_enter.1, bf16[1,8,3584]{2,1,0:T(8,128)(2,1)} %bwd_in.1, bf16[1,8,3584]{2,1,0:T(8,128)(2,1)} %bwd_enter.1, bf16[1,2,8,3584]{3,2,1,0:T(8,128)(2,1)} %saved.1, ...), custom_call_target="tpu_custom_call" | custom-call | tf_op jit(solution)/shard_map/relay/pallas_call | solution.py:533
  74.6 1.7 %store.1 = (bf16[1,2,8,3584]{3,2,1,0:T(8,128)(2,1)}, bf16[1,2,8,3584]{3,2,1,0:T(8,128)(2,1)}) custom-call(bf16[1,2,8,3584]{3,2,1,0:T(8,128)(2,1)} %get-tuple-element.4.fwd, bf16[1,2,8,3584]{3,2,1,0:T(8,128)(2,1)} %get-tuple-element.5.bwd), custom_call_target="tpu_custom_call" | custom-call | tf_op jit(solution)/shard_map/store/pallas_call | solution.py:555

commit v4 on v3

--- a/solution.py
+++ b/solution.py
@@ -51,6 +51,7 @@
     gain_v,
     w_in,
     w_back,
+    w_in_turned,
     line_y,
     line_x,
     packed_x,
@@ -135,7 +136,10 @@
     loads[1].wait()
     loads[2].wait()
     gain_row = gain_v[...]
+    quarter = half // 2
     first, second = pl.ds(0, half), pl.ds(half, half)
+    parts = [pl.ds(c * quarter, quarter) for c in range(2)]
+    second_parts = [pl.ds(half + c * quarter, quarter) for c in range(2)]
 
     def place_own(u, block):
         line_y[u, y] = block[:, :half]
@@ -275,53 +279,62 @@
     def turn_rows(array):
         return jnp.dot(turn, array, preferred_element_type=F32).astype(BF16)
 
-    def reduce_x(u):
+    def reduce_x(u, c):
         out = []
         for k, step in enumerate(PEERS):
-            source, target = partial_x.at[u, lax.rem(x + step, SIDE)], landed_x.at[u, k]
-            out.append(remote(source, target, reduce_send, reduce_recv, (u, 0, 0, k), along_x[k]))
+            source = partial_x.at[u, lax.rem(x + step, SIDE), :, :, parts[c]]
+            target = landed_x.at[u, k, :, :, parts[c]]
+            index = (u, 0, 0, c, k)
+            out.append(remote(source, target, reduce_send, reduce_recv, index, along_x[k]))
         return start(out)
 
-    def reduce_y(u):
+    def reduce_y(u, c):
         out = []
         for k, step in enumerate(PEERS):
-            source, target = partial_y.at[u, lax.rem(y + step, SIDE)], landed_y.at[u, y]
-            out.append(remote(source, target, reduce_send, reduce_recv, (u, 0, 1, k), along_y[k]))
+            source = partial_y.at[u, lax.rem(y + step, SIDE), :, :, parts[c]]
+            target = landed_y.at[u, y, :, :, parts[c]]
+            index = (u, 0, 1, c, k)
+            out.append(remote(source, target, reduce_send, reduce_recv, index, along_y[k]))
         start(out)
-        landed_y[u, y] = partial_y[u, y]
+        landed_y[u, y, :, :, parts[c]] = partial_y[u, y, :, :, parts[c]]
         return out
 
     transposed = (((0,), (0,)), ((), ()))
 
-    def last_leg(u, part, at, peers):
+    def last_leg(u, part, c, at, peers):
         out = []
         for k, step in enumerate(PEERS):
-            source, target = middle.at[u, part, lax.rem(at + step, SIDE)], landed_two.at[u, part, k]
-            out.append(remote(source, target, reduce_send, reduce_recv, (u, 1, part, k), peers[k]))
+            source = middle.at[u, part, lax.rem(at + step, SIDE), :, parts[c]]
+            target = landed_two.at[u, part, k, :, parts[c]]
+            index = (u, 1, part, c, k)
+            out.append(remote(source, target, reduce_send, reduce_recv, index, peers[k]))
         return start(out)
 
     def reduce_two(u, r, ones):
-        arrive(ones[0])
-        total = partial_x[u, x].astype(F32)
-        for k in range(len(PEERS)):
-            total = total + landed_x[u, k].astype(F32)
-        spread = lax.dot_general(
-            pick_x[r].astype(BF16),
-            total.astype(BF16).reshape(slots, half),
-            transposed,
-            preferred_element_type=F32,
-        )
-        middle[u, 0] = spread.astype(BF16).reshape(SIDE, rows, half)
-        across_y = last_leg(u, 0, y, along_y)
-        arrive(ones[1])
-        spread = lax.dot_general(
-            pick_y[r].astype(BF16),
-            landed_y[u].reshape(whole, half),
-            transposed,
-            preferred_element_type=F32,
-        )
-        middle[u, 1] = spread.astype(BF16).reshape(SIDE, rows, half)
-        return across_y + last_leg(u, 1, x, along_x)
+        out = []
+        for c in range(2):
+            arrive(ones[c][0])
+            total = partial_x[u, x, :, :, parts[c]].astype(F32)
+            for k in range(len(PEERS)):
+                total = total + landed_x[u, k, :, :, parts[c]].astype(F32)
+            spread = lax.dot_general(
+                pick_x[r].astype(BF16),
+                total.astype(BF16).reshape(slots, quarter),
+                transposed,
+                preferred_element_type=F32,
+            )
+            middle[u, 0, :, :, parts[c]] = spread.astype(BF16).reshape(SIDE, rows, quarter)
+            out += last_leg(u, 0, c, y, along_y)
+            arrive(ones[c][1])
+            spread = lax.dot_general(
+                pick_y[r].astype(BF16),
+                landed_y[u, :, :, :, parts[c]].reshape(whole, quarter),
+                transposed,
+                preferred_element_type=F32,
+            )
+            middle[u, 1, :, :, parts[c]] = spread.astype(BF16).reshape(SIDE, rows, quarter)
+            out += last_leg(u, 1, c, x, along_x)
+        return out
 
     def reduce_end(u):
         sums = []
@@ -338,17 +351,21 @@
         arrive(twos[1])
         return both + jnp.dot(by_row(u), w_in[second, :], preferred_element_type=F32)
 
-    shape = (SIDE, tiles, rows, half)
+    shape = (SIDE, tiles, rows, quarter)
 
     def forward(target, r, both):
         a, up = both[:, : 2 * unit], both[:, 2 * unit :]
         hidden = (a / (1.0 + jnp.exp(-a)) * up * weight_of[r]).astype(BF16)
-        piece = jnp.dot(hidden, w_back[:, first], preferred_element_type=F32)
-        partial_x[target] = piece.astype(BF16).reshape(shape)
-        across_x = reduce_x(target)
-        piece = jnp.dot(turn_rows(hidden), w_back[:, second], preferred_element_type=F32)
-        partial_y[target] = piece.astype(BF16).reshape(shape)
-        return across_x, reduce_y(target)
+        hidden_turned = turn_rows(hidden)
+        out = []
+        for c in range(2):
+            piece = jnp.dot(hidden, w_back[:, parts[c]], preferred_element_type=F32)
+            partial_x[target, :, :, :, parts[c]] = piece.astype(BF16).reshape(shape)
+            across_x = reduce_x(target, c)
+            piece = jnp.dot(hidden_turned, w_back[:, second_parts[c]], preferred_element_type=F32)
+            partial_y[target, :, :, :, parts[c]] = piece.astype(BF16).reshape(shape)
+            out.append((across_x, reduce_y(target, c)))
+        return out
 
     contract = (((1,), (1,)), ((), ()))
 
@@ -367,14 +384,29 @@
         d_gate = (d_hidden * up * sigma * (1.0 + a * (1.0 - sigma))).astype(BF16)
         d_up = (d_hidden * a * sigma).astype(BF16)
         grads = jnp.concatenate([d_gate, d_up], axis=-1)
-        piece = lax.dot_general(grads, w_in[first, :], contract, preferred_element_type=F32)
-        partial_x[target] = piece.astype(BF16).reshape(shape)
-        across_x = reduce_x(target)
-        piece = lax.dot_general(
-            turn_rows(grads), w_in[second, :], contract, preferred_element_type=F32
-        )
-        partial_y[target] = piece.astype(BF16).reshape(shape)
-        return across_x, reduce_y(target)
+        grads_turned = turn_rows(grads)
+        out = []
+        for c in range(2):
+            piece = jnp.dot(grads, w_in_turned[:, parts[c]], preferred_element_type=F32)
+            partial_x[target, :, :, :, parts[c]] = piece.astype(BF16).reshape(shape)
+            across_x = reduce_x(target, c)
+            piece = jnp.dot(grads_turned, w_in_turned[:, second_parts[c]], preferred_element_type=F32)
+            partial_y[target, :, :, :, parts[c]] = piece.astype(BF16).reshape(shape)
+            out.append((across_x, reduce_y(target, c)))
+        return out
+
+    def turn_weights():
+        span = 2 * unit
+        eye = jnp.where(iota((span, span), 0) == iota((span, span), 1), 1.0, 0.0).astype(BF16)
+        for i in range(2):
+            for rows_of in (first, second):
+                turned_part = lax.dot_general(
+                    eye,
+                    w_in[rows_of, pl.ds(i * span, span)],
+                    contract,
+                    preferred_element_type=F32,
+                )
+                w_in_turned[pl.ds(i * span, span), rows_of] = turned_part.astype(BF16)
 
     def forward_end(u, inputs):
         return (inputs.astype(F32) + reduce_end(u)).astype(BF16)
@@ -414,25 +446,26 @@
     gather_s = gather_two(1, 2, gather_s)
     gather_g = gather_two(2, 2, gather_g)
     gather_f = gather_two(0, 0, gather_f)
+    gather_n = start(gather_one(4))
     for load in loads[len(small) :]:
         load.wait()
     arrive(weights)
+    turn_weights()
     both = pre_activation(1, gather_s)
     reduce_b = backward(2, 1, both, 2, gather_g)
     both = pre_activation(0, gather_f)
     reduce_f = forward(0, 0, both)
-    gather_n = start(gather_one(4))
     reduce_b = reduce_two(1, 2, reduce_b)
     reduce_f = reduce_two(0, 0, reduce_f)
+    gather_n = gather_two(4, 3, gather_n)
     arrive(reduce_b)
     outputs = backward_end(1, 0, in_b[...])
     hop_b = hop(1, outputs, preceding)
-    bwd_out[0, 0] = outputs
-    gather_n = gather_two(4, 3, gather_n)
     arrive(reduce_f)
     outputs = forward_end(0, in_f[...])
     hop_f = hop(0, outputs, following)
-    fwd_out[0, 0] = outputs
+    bwd_out[0, 0] = hop_send[1]
+    fwd_out[0, 0] = hop_send[0]
 
     arrive(hop_b)
     moved_b = jnp.where(
@@ -445,9 +478,9 @@
     _, normed = normalize(moved_f, gain_row)
     place_own(3, normed)
     gather_f = start(gather_one(3))
-    pre_act[...] = pre_activation(4, gather_n)
     gather_g = gather_two(5, 3, gather_g)
     gather_f = gather_two(3, 1, gather_f)
+    pre_act[...] = pre_activation(4, gather_n)
     reduce_b = backward(5, 3, pre_act[...], 3, gather_g)
     both = pre_activation(3, gather_f)
     reduce_f = forward(2, 1, both)
@@ -502,6 +535,7 @@
         pltpu.VMEM((1, width), F32),
         pltpu.VMEM((width, 4 * unit), BF16),
         pltpu.VMEM((2 * unit, width), BF16),
+        pltpu.VMEM((4 * unit, width), BF16),
         pltpu.VMEM((6, SIDE, rows, half), BF16),
         pltpu.VMEM((6, SIDE, rows, half), BF16),
         pltpu.VMEM((6, SIDE, tiles, rows, half), BF16),
@@ -524,8 +558,8 @@
         dma((3,)),
         dma((6, 2, 2, peers)),
         dma((6, 2, 2, peers)),
-        dma((4, 2, 2, peers)),
-        dma((4, 2, 2, peers)),
+        dma((4, 2, 2, 2, peers)),
+        dma((4, 2, 2, 2, peers)),
         dma((2,)),
         dma((2,)),
     ]

time: 76.4 us -> 75.4 us (0.987)
  Pallas kernels: 75.6 us -> 74.6 us
    pallas_call x1, Pallas kernels: 73.9 us -> 72.9 us  [per_device(): pl.pallas_call(functools.partial(relay_kernel, sections), out_shape=(out,...]
where the time goes in v4:
time: 75.4 us; the launch traced here: 75.2 us
  Pallas kernels  74.6 us (99%)
    pallas_call x1, Pallas kernels, per_device(): pl.pallas_call(functools.partial(relay_kernel, sections), out_shape=(out,...  72.9 us
    pallas_call x1, Pallas kernels, per_device(): pl.pallas_call(store_kernel, out_shape=(out, out), in_specs=[pl.BlockSpec...  1.65 us

profile of v4, /device:TPU:8, one launch (start us, length us, event | category | flops | bytes accessed | tf_op | source)
XLA Modules:
  0.0 75.2 jit_solution(18019549118539993144)
XLA Ops:
  0.6 72.9 %relay.1 = (bf16[1,2,8,3584]{3,2,1,0:T(8,128)(2,1)}, bf16[1,2,8,3584]{3,2,1,0:T(8,128)(2,1)}) custom-call(bf16[1,8,3584]{2,1,0:T(8,128)(2,1)} %fwd_in.1, bf16[1,8,3584]{2,1,0:T(8,128)(2,1)} %fwd_enter.1, bf16[1,8,3584]{2,1,0:T(8,128)(2,1)} %bwd_in.1, bf16[1,8,3584]{2,1,0:T(8,128)(2,1)} %bwd_enter.1, bf16[1,2,8,3584]{3,2,1,0:T(8,128)(2,1)} %saved.1, ...), custom_call_target="tpu_custom_call" | custom-call | tf_op jit(solution)/shard_map/relay/pallas_call | solution.py:567
  73.5 1.7 %store.1 = (bf16[1,2,8,3584]{3,2,1,0:T(8,128)(2,1)}, bf16[1,2,8,3584]{3,2,1,0:T(8,128)(2,1)}) custom-call(bf16[1,2,8,3584]{3,2,1,0:T(8,128)(2,1)} %get-tuple-element.4.fwd, bf16[1,2,8,3584]{3,2,1,0:T(8,128)(2,1)} %get-tuple-element.5.bwd), custom_call_target="tpu_custom_call" | custom-call | tf_op jit(solution)/shard_map/store/pallas_call | solution.py:589

commit v5 on v3

--- a/solution.py
+++ b/solution.py
@@ -51,6 +51,7 @@
     gain_v,
     w_in,
     w_back,
+    w_in_turned,
     line_y,
     line_x,
     packed_x,
@@ -367,14 +368,25 @@
         d_gate = (d_hidden * up * sigma * (1.0 + a * (1.0 - sigma))).astype(BF16)
         d_up = (d_hidden * a * sigma).astype(BF16)
         grads = jnp.concatenate([d_gate, d_up], axis=-1)
-        piece = lax.dot_general(grads, w_in[first, :], contract, preferred_element_type=F32)
+        piece = jnp.dot(grads, w_in_turned[:, first], preferred_element_type=F32)
         partial_x[target] = piece.astype(BF16).reshape(shape)
         across_x = reduce_x(target)
-        piece = lax.dot_general(
-            turn_rows(grads), w_in[second, :], contract, preferred_element_type=F32
-        )
+        piece = jnp.dot(turn_rows(grads), w_in_turned[:, second], preferred_element_type=F32)
         partial_y[target] = piece.astype(BF16).reshape(shape)
         return across_x, reduce_y(target)
+
+    def turn_weights():
+        span = 2 * unit
+        eye = jnp.where(iota((span, span), 0) == iota((span, span), 1), 1.0, 0.0).astype(BF16)
+        for i in range(2):
+            for rows_of in (first, second):
+                turned_part = lax.dot_general(
+                    eye,
+                    w_in[rows_of, pl.ds(i * span, span)],
+                    contract,
+                    preferred_element_type=F32,
+                )
+                w_in_turned[pl.ds(i * span, span), rows_of] = turned_part.astype(BF16)
 
     def forward_end(u, inputs):
         return (inputs.astype(F32) + reduce_end(u)).astype(BF16)
@@ -414,25 +426,26 @@
     gather_s = gather_two(1, 2, gather_s)
     gather_g = gather_two(2, 2, gather_g)
     gather_f = gather_two(0, 0, gather_f)
+    gather_n = start(gather_one(4))
     for load in loads[len(small) :]:
         load.wait()
     arrive(weights)
+    turn_weights()
     both = pre_activation(1, gather_s)
     reduce_b = backward(2, 1, both, 2, gather_g)
     both = pre_activation(0, gather_f)
     reduce_f = forward(0, 0, both)
-    gather_n = start(gather_one(4))
     reduce_b = reduce_two(1, 2, reduce_b)
     reduce_f = reduce_two(0, 0, reduce_f)
+    gather_n = gather_two(4, 3, gather_n)
     arrive(reduce_b)
     outputs = backward_end(1, 0, in_b[...])
     hop_b = hop(1, outputs, preceding)
-    bwd_out[0, 0] = outputs
-    gather_n = gather_two(4, 3, gather_n)
     arrive(reduce_f)
     outputs = forward_end(0, in_f[...])
     hop_f = hop(0, outputs, following)
-    fwd_out[0, 0] = outputs
+    bwd_out[0, 0] = hop_send[1]
+    fwd_out[0, 0] = hop_send[0]
 
     arrive(hop_b)
     moved_b = jnp.where(
@@ -445,8 +458,8 @@
     _, normed = normalize(moved_f, gain_row)
     place_own(3, normed)
     gather_f = start(gather_one(3))
+    gather_g = gather_two(5, 3, gather_g)
     pre_act[...] = pre_activation(4, gather_n)
-    gather_g = gather_two(5, 3, gather_g)
     gather_f = gather_two(3, 1, gather_f)
     reduce_b = backward(5, 3, pre_act[...], 3, gather_g)
     both = pre_activation(3, gather_f)
@@ -502,6 +515,7 @@
         pltpu.VMEM((1, width), F32),
         pltpu.VMEM((width, 4 * unit), BF16),
         pltpu.VMEM((2 * unit, width), BF16),
+        pltpu.VMEM((4 * unit, width), BF16),
         pltpu.VMEM((6, SIDE, rows, half), BF16),
         pltpu.VMEM((6, SIDE, rows, half), BF16),
         pltpu.VMEM((6, SIDE, tiles, rows, half), BF16),

time: 76.4 us -> 74.8 us (0.979)
  the two profiles are of different devices: /device:TPU:8 before, /device:TPU:2 now
where the time goes in v5:
time: 74.8 us; the launch traced here: 74.6 us
  Pallas kernels  74 us (99%)
    pallas_call x1, Pallas kernels, per_device(): pl.pallas_call(functools.partial(relay_kernel, sections), out_shape=(out,...  72.3 us
    pallas_call x1, Pallas kernels, per_device(): pl.pallas_call(store_kernel, out_shape=(out, out), in_specs=[pl.BlockSpec...  1.65 us

profile of v5, /device:TPU:2, one launch (start us, length us, event | category | flops | bytes accessed | tf_op | source)
XLA Modules:
  0.0 74.6 jit_solution(2986399347881068310)
XLA Ops:
  0.6 72.3 %relay.1 = (bf16[1,2,8,3584]{3,2,1,0:T(8,128)(2,1)}, bf16[1,2,8,3584]{3,2,1,0:T(8,128)(2,1)}) custom-call(bf16[1,8,3584]{2,1,0:T(8,128)(2,1)} %fwd_in.1, bf16[1,8,3584]{2,1,0:T(8,128)(2,1)} %fwd_enter.1, bf16[1,8,3584]{2,1,0:T(8,128)(2,1)} %bwd_in.1, bf16[1,8,3584]{2,1,0:T(8,128)(2,1)} %bwd_enter.1, bf16[1,2,8,3584]{3,2,1,0:T(8,128)(2,1)} %saved.1, ...), custom_call_target="tpu_custom_call" | custom-call | tf_op jit(solution)/shard_map/relay/pallas_call | solution.py:547
  72.9 1.7 %store.1 = (bf16[1,2,8,3584]{3,2,1,0:T(8,128)(2,1)}, bf16[1,2,8,3584]{3,2,1,0:T(8,128)(2,1)}) custom-call(bf16[1,2,8,3584]{3,2,1,0:T(8,128)(2,1)} %get-tuple-element.4.fwd, bf16[1,2,8,3584]{3,2,1,0:T(8,128)(2,1)} %get-tuple-element.5.bwd), custom_call_target="tpu_custom_call" | custom-call | tf_op jit(solution)/shard_map/store/pallas_call | solution.py:569

commit v6 on v5

--- a/solution.py
+++ b/solution.py
@@ -458,9 +458,13 @@
     _, normed = normalize(moved_f, gain_row)
     place_own(3, normed)
     gather_f = start(gather_one(3))
+    done = list(sent)
+    sent.clear()
     gather_g = gather_two(5, 3, gather_g)
     pre_act[...] = pre_activation(4, gather_n)
     gather_f = gather_two(3, 1, gather_f)
+    for copy in done:
+        copy.wait_send()
     reduce_b = backward(5, 3, pre_act[...], 3, gather_g)
     both = pre_activation(3, gather_f)
     reduce_f = forward(2, 1, both)

time: 74.8 us -> 74.6 us (level)
  no operation moved by 1% of the time
where the time goes in v6:
time: 74.6 us; the launch traced here: 74.5 us
  Pallas kernels  73.8 us (99%)
    pallas_call x1, Pallas kernels, per_device(): pl.pallas_call(functools.partial(relay_kernel, sections), out_shape=(out,...  72.2 us
    pallas_call x1, Pallas kernels, per_device(): pl.pallas_call(store_kernel, out_shape=(out, out), in_specs=[pl.BlockSpec...  1.65 us

profile of v6, /device:TPU:2, one launch (start us, length us, event | category | flops | bytes accessed | tf_op | source)
XLA Modules:
  0.0 74.5 jit_solution(13844706436688999631)
XLA Ops:
  0.6 72.2 %relay.1 = (bf16[1,2,8,3584]{3,2,1,0:T(8,128)(2,1)}, bf16[1,2,8,3584]{3,2,1,0:T(8,128)(2,1)}) custom-call(bf16[1,8,3584]{2,1,0:T(8,128)(2,1)} %fwd_in.1, bf16[1,8,3584]{2,1,0:T(8,128)(2,1)} %fwd_enter.1, bf16[1,8,3584]{2,1,0:T(8,128)(2,1)} %bwd_in.1, bf16[1,8,3584]{2,1,0:T(8,128)(2,1)} %bwd_enter.1, bf16[1,2,8,3584]{3,2,1,0:T(8,128)(2,1)} %saved.1, ...), custom_call_target="tpu_custom_call" | custom-call | tf_op jit(solution)/shard_map/relay/pallas_call | solution.py:551
  72.8 1.7 %store.1 = (bf16[1,2,8,3584]{3,2,1,0:T(8,128)(2,1)}, bf16[1,2,8,3584]{3,2,1,0:T(8,128)(2,1)}) custom-call(bf16[1,2,8,3584]{3,2,1,0:T(8,128)(2,1)} %get-tuple-element.4.fwd, bf16[1,2,8,3584]{3,2,1,0:T(8,128)(2,1)} %get-tuple-element.5.bwd), custom_call_target="tpu_custom_call" | custom-call | tf_op jit(solution)/shard_map/store/pallas_call | solution.py:573
